TPU v7x, 512 devices: a whole 4x8x8 slice. The times are simulated.
512 devices in a mesh: tm: 64 (over z, x, core), space: 8 (over y).
Axes of the slice: x: 4, y: 8, z: 8, core: 2. Of those that a mesh axis runs over, the one named last changes fastest.
Arguments:
- nodes: float32 [64, 2, 2, 32, 128, 128], P('tm', None, None, 'space'), may hold values from -3 to 3
- initial: float32 [2, 32, 128, 128], P(None, 'space'), may hold values from -3 to 3
Outputs:
- corrected: float32 [64, 2, 2, 32, 128, 128], P('tm', None, None, 'space')
All inputs are finite; a program needn't handle non-finite values.
Results may differ from a plain program's by a relative error of at most 0.0003.
Values sent between devices are 32-bit elements; how exact they have to be, the bound alone decides.
A program may use at most 128 MiB of HBM per device.

v0:
```python
import math

import jax
import jax.numpy as jnp
from jax import lax
from jax.sharding import PartitionSpec as P

diffuse_fast = 0.5
diffuse_slow = 0.25
feed_rate = 0.04
kill_rate = 0.06
slice_length = 0.5
node_step = 0.25
sweep_weights = ((5.0 / 24.0, 1.0 / 3.0, -1.0 / 24.0), (-1.0 / 24.0, 1.0 / 3.0, 5.0 / 24.0))


def with_halo(x, sides, width):
    for axis, dim in sides:
        devices, length = (lax.axis_size(axis), x.shape[dim])
        up = [(i, (i + 1) % devices) for i in range(devices - 1)]
        down = [(j, i) for i, j in up]
        last = lax.slice_in_dim(x, length - width, length, axis=dim)
        leading = lax.slice_in_dim(x, 0, width, axis=dim)
        before = lax.ppermute(last, axis, up)
        after = lax.ppermute(leading, axis, down)
        x = jnp.concatenate([before, x, after], axis=dim)
    return x


def passed_along(value, axis, steps):
    count = lax.axis_size(axis)
    leading, last = (max(0, -steps), min(count, count - steps))
    return lax.ppermute(value, axis, [(source, source + steps) for source in range(leading, last)])


def entering(value, axis, join, neutral):
    count, mine = (lax.axis_size(axis), lax.axis_index(axis))
    pieces = jax.tree.map(lambda part: lax.all_gather(part, axis), value)
    subtotal = jax.tree.map(
        lambda part, zero: jnp.full_like(part, 0) + jnp.asarray(zero, part.dtype), value, neutral
    )

    def lap(position, subtotal):
        longer = join(subtotal, jax.tree.map(lambda part: part[position], pieces))
        return jax.tree.map(lambda new, old: jnp.where(position < mine, new, old), longer, subtotal)

    return lax.fori_loop(0, count - 1, lap, subtotal)


def sine_table(points, modes, stretch):
    place = jnp.arange(points).astype(jnp.float32) + 0.5
    order = jnp.arange(modes).astype(jnp.float32) + 1.0
    angle = math.pi / (stretch * modes) * place[:, None] * order[None, :]
    weight = jnp.where(jnp.arange(modes) == modes - 1, math.sqrt(0.5), 1.0).astype(jnp.float32)
    return math.sqrt(2.0 / modes) * weight[None, :] * jnp.sin(angle)


def tendency(values):
    center = values[..., 1:-1, :, :]
    padded = jnp.pad(center, [(0, 0)] * (center.ndim - 2) + [(1, 1), (1, 1)])
    laplace = (
        values[..., 2:, :, :]
        + values[..., :-2, :, :]
        + padded[..., 2:, 1:-1]
        + padded[..., :-2, 1:-1]
    )
    laplace = laplace + padded[..., 1:-1, 2:] + padded[..., 1:-1, :-2] - 6.0 * center
    first_kind = center[..., 0, :, :, :]
    second_kind = center[..., 1, :, :, :]
    reaction = (1.0 + first_kind) * second_kind * second_kind
    first_rate = diffuse_fast * laplace[..., 0, :, :, :] - reaction - feed_rate * first_kind
    second_rate = (
        diffuse_slow * laplace[..., 1, :, :, :] + reaction - (feed_rate + kill_rate) * second_kind
    )
    return jnp.stack([first_rate, second_rate], axis=-4)


def restrict(values):
    shape = values.shape
    blocks = values.reshape(shape[:-3] + (shape[-3] // 2, 2, shape[-2] // 2, 2, shape[-1] // 2, 2))
    return jnp.mean(blocks, axis=(-5, -3, -1))


def with_rims(values):
    return with_halo(values, (("space", 2),), 1)


def join_pairs(earlier, later):
    return (earlier[0] * later[0], later[0] * earlier[1] + later[1])


def local(nodes, initial):
    planes_dev = initial.shape[1]
    width_x = initial.shape[2]
    width_y = initial.shape[3]
    spaces = lax.axis_size("space")
    modes_x = width_x // 2
    modes_y = width_y // 2
    modes_z = planes_dev * spaces // 2
    columns = modes_x * modes_y // spaces
    highest = lax.Precision.HIGHEST
    (w00, w01, w02), (w10, w11, w12) = sweep_weights
    own_nodes = nodes[0]
    prior_end = passed_along(own_nodes[1], "tm", 1)
    is_first = lax.axis_index("tm") == 0
    start_value = jnp.where(is_first, initial, prior_end)
    stacked = jnp.stack([start_value, own_nodes[0], own_nodes[1]])
    slopes = tendency(with_rims(stacked))
    swept_one = start_value + slice_length * (w00 * slopes[0] + w01 * slopes[1] + w02 * slopes[2])
    slope_one = tendency(with_rims(swept_one[None]))[0]
    swept_two = (
        swept_one
        + node_step * (slope_one - slopes[1])
        + slice_length * (w10 * slopes[0] + w11 * slopes[1] + w12 * slopes[2])
    )
    slope_two = tendency(with_rims(swept_two[None]))[0]
    integral_one = slice_length * (w00 * slopes[0] + w01 * slope_one + w02 * slope_two)
    integral_two = slice_length * (w10 * slopes[0] + w11 * slope_one + w12 * slope_two)
    coarse = restrict(jnp.stack([integral_one, integral_two, start_value, swept_one, swept_two]))
    forward_x = sine_table(modes_x, modes_x, 1.0).T
    forward_y = sine_table(modes_y, modes_y, 1.0).T
    forward_z = sine_table(modes_z, modes_z, 1.0).T
    along_y = jnp.einsum("by,fszxy->fszxb", forward_y, coarse, precision=highest)
    spectra_xy = jnp.einsum("ax,fszxb->fszab", forward_x, along_y, precision=highest)
    spectra_xy = spectra_xy.reshape(5, 2, planes_dev // 2, modes_x * modes_y)
    gathered = lax.all_to_all(spectra_xy, "space", split_axis=3, concat_axis=2, tiled=True)
    spectra = jnp.einsum("kz,fszc->fskc", forward_z, gathered, precision=highest)
    column_ids = lax.axis_index("space") * columns + jnp.arange(columns)
    order_x = (column_ids // modes_y + 1).astype(jnp.float32)
    order_y = (column_ids % modes_y + 1).astype(jnp.float32)
    order_z = jnp.arange(modes_z).astype(jnp.float32) + 1.0
    eigen_xy = (
        2.0 * jnp.cos(math.pi * order_x / modes_x)
        - 2.0
        + 2.0 * jnp.cos(math.pi * order_y / modes_y)
        - 2.0
    )
    eigen_z = 2.0 * jnp.cos(math.pi * order_z / modes_z) - 2.0
    eigen_sum = (eigen_z[:, None] + eigen_xy[None, :]) / 4.0
    linear = jnp.stack(
        [diffuse_fast * eigen_sum - feed_rate, diffuse_slow * eigen_sum - (feed_rate + kill_rate)]
    )
    factor = 1.0 / (1.0 - node_step * linear)
    remain_one = spectra[0] - node_step * linear * spectra[3]
    remain_two = spectra[1] - node_step * linear * spectra[4]
    seed_value = jnp.where(is_first, spectra[2], 0.0)
    element = factor * (factor * (seed_value + remain_one) + remain_two)
    _, prefix = entering(
        (factor * factor, element),
        "tm",
        join_pairs,
        (jnp.ones_like(element), jnp.zeros_like(element)),
    )
    start_hat = jnp.where(is_first, spectra[2], prefix)
    new_one = factor * (start_hat + remain_one)
    new_two = factor * (new_one + remain_two)
    change = jnp.stack([new_one - spectra[3], new_two - spectra[4]])
    interp_x = sine_table(width_x, modes_x, 2.0)
    interp_y = sine_table(width_y, modes_y, 2.0)
    interp_z = sine_table(planes_dev * spaces, modes_z, 2.0)
    at_planes = jnp.einsum("zk,fskc->fszc", interp_z, change, precision=highest)
    returned = lax.all_to_all(at_planes, "space", split_axis=2, concat_axis=3, tiled=True)
    returned = returned.reshape(2, 2, planes_dev, modes_x, modes_y)
    widened_y = jnp.einsum("yb,fszab->fszay", interp_y, returned, precision=highest)
    refined = jnp.einsum("xa,fszay->fszxy", interp_x, widened_y, precision=highest)
    corrected = jnp.stack([swept_one + refined[0], swept_two + refined[1]])
    return corrected[None]


def solution(mesh):
    in_specs = (P("tm", None, None, "space", None, None), P(None, "space", None, None))
    out_specs = P("tm", None, None, "space", None, None)
    return jax.shard_map(local, mesh=mesh, in_specs=in_specs, out_specs=out_specs, check_vma=False)
```

profile of v0, /device:TPU:1, one launch (start us, length us, event | category | flops | bytes accessed | tf_op | source)
XLA Modules:
  0.0 693.1 jit_solution(5441108062914970493)
XLA Ops:
  6.5 1.3 fusion.109
  8.1 4.5 collective-permute-start
  13.0 5.7 collective-permute-done
  18.9 1.3 collective-permute-start.1
  20.2 4.0 collective-permute-start.2
  24.2 7.0 %collective-permute-done.1 = f32[3,2,1,128,128]{3,4,2,1,0:T(8,128)S(1)} collective-permute-done((f32[3,2,1,128,128]{3,4,2,1,0:T(8,128)S(1)}, f32[3,2,1,128,128]{3,4,2,1,0:T(8,128)S(1)}, u32[]{:S(2)}, u32[]{:S(2)}) %collective-permute-start.1) | collective-permute-done | bytes 393248 | tf_op jit(solution)/shard_map/ppermute | solution.py:25
  31.2 1.8 collective-permute-done.2
  33.0 0.9 fusion.5
  34.5 1.3 collective-permute-start.3
  35.8 4.5 collective-permute-start.4
  40.3 1.6 collective-permute-done.3
  44.6 1.3 collective-permute-start.5
  45.9 5.4 collective-permute-start.6
  51.3 34.8 %reshape.460 = f32[1,2,2,2,64,2,64,2]{5,4,7,6,3,2,1,0:T(8,128)} reshape(f32[2,4,128,128]{2,3,1,0:T(8,128)S(1)} %broadcast_select_fusion) | data formatting | bytes 1048576 | tf_op jit(solution)/shard_map/stack | solution.py:119
  86.2 22.8 %copy.49 = f32[1,2,2,2,64,2,64,2]{6,4,7,5,3,2,1,0:T(8,128)S(1)} copy(f32[1,2,2,2,64,2,64,2]{5,4,7,6,3,2,1,0:T(8,128)} %reshape.460) | data formatting | bytes 1048576 | tf_op jit(solution)/shard_map/stack | solution.py:119
  109.0 34.9 %reshape.461 = f32[1,2,2,2,64,2,64,2]{5,4,7,6,3,2,1,0:T(8,128)} reshape(f32[2,4,128,128]{2,3,1,0:T(8,128)S(1)} %get-tuple-element.130) | data formatting | bytes 1048576 | tf_op jit(solution)/shard_map/stack | solution.py:119
  143.9 23.8 %copy.50 = f32[1,2,2,2,64,2,64,2]{6,4,7,5,3,2,1,0:T(8,128)} copy(f32[1,2,2,2,64,2,64,2]{5,4,7,6,3,2,1,0:T(8,128)} %reshape.461) | data formatting | bytes 1048576 | tf_op jit(solution)/shard_map/stack | solution.py:119
  167.6 34.8 %reshape.462 = f32[1,2,2,2,64,2,64,2]{5,4,7,6,3,2,1,0:T(8,128)} reshape(f32[2,4,128,128]{2,3,1,0:T(8,128)S(1)} %bitcast_add_fusion.1) | data formatting | bytes 1048576 | tf_op jit(solution)/shard_map/stack | solution.py:119
  202.5 23.8 %copy.51 = f32[1,2,2,2,64,2,64,2]{6,4,7,5,3,2,1,0:T(8,128)} copy(f32[1,2,2,2,64,2,64,2]{5,4,7,6,3,2,1,0:T(8,128)} %reshape.462) | data formatting | bytes 1048576 | tf_op jit(solution)/shard_map/stack | solution.py:119
  226.3 1.3 fusion.22
  227.7 1.2 add_multiply_fusion
  228.9 35.6 %reshape.458 = f32[1,2,2,2,64,2,64,2]{5,4,7,6,3,2,1,0:T(8,128)} reshape(f32[1,2,4,128,128]{3,4,2,1,0:T(8,128)} %get-tuple-element.135) | data formatting | bytes 1048576 | tf_op jit(solution)/shard_map/stack | solution.py:119
  264.5 22.8 %copy.47 = f32[1,2,2,2,64,2,64,2]{6,4,7,5,3,2,1,0:T(8,128)S(1)} copy(f32[1,2,2,2,64,2,64,2]{5,4,7,6,3,2,1,0:T(8,128)} %reshape.458) | data formatting | bytes 1048576 | tf_op jit(solution)/shard_map/stack | solution.py:119
  287.3 1.1 constant_dynamic-update-slice_fusion.4
  288.4 35.6 %reshape.459 = f32[1,2,2,2,64,2,64,2]{5,4,7,6,3,2,1,0:T(8,128)} reshape(f32[1,2,4,128,128]{3,4,2,1,0:T(8,128)} %get-tuple-element.134) | data formatting | bytes 1048576 | tf_op jit(solution)/shard_map/stack | solution.py:119
  324.0 23.0 %copy.48 = f32[1,2,2,2,64,2,64,2]{6,4,7,5,3,2,1,0:T(8,128)S(1)} copy(f32[1,2,2,2,64,2,64,2]{5,4,7,6,3,2,1,0:T(8,128)} %reshape.459) | data formatting | bytes 1048576 | tf_op jit(solution)/shard_map/stack | solution.py:119
  347.0 1.1 constant_dynamic-update-slice_fusion.3
  348.1 1.1 constant_dynamic-update-slice_fusion.2
  349.7 1.1 constant_dynamic-update-slice_fusion.1
  351.3 1.1 constant_dynamic-update-slice_fusion
  352.4 3.2 reduce_sum.9
  355.6 2.2 fusion.11
  358.6 9.2 %copy.74 = f32[5,2,2,64,64]{0,2,1,4,3:T(2,128)} copy(f32[5,2,2,64,64]{3,4,2,1,0:T(8,128)S(1)} %convolution_bitcast_fusion.1) | data formatting | bytes 655360 | tf_op jit(solution)/shard_map/reshape | solution.py:125
  367.9 13.3 %reshape.463 = f32[8,1,10240]{2,1,0:T(1,128)} reshape(f32[4096,2,2,5]{3,2,1,0:T(2,128)} %bitcast.158) | data formatting | bytes 655360
  381.1 4.4 all-to-all-start
  385.8 10.6 %all-to-all-done = f32[8,1,10240]{2,1,0:T(1,128)S(1)} async-done(((f32[8,1,10240]{2,1,0:T(1,128)}), f32[8,1,10240]{2,1,0:T(1,128)S(1)}, u32[]{:S(2)}, u32[]{:S(2)}) %all-to-all-start) | async-done | bytes 327712 | tf_op jit(solution)/shard_map/all_to_all | solution.py:126
  396.9 1.4 reduce
  398.3 16.4 %reshape.464 = f32[4096,2,2,5]{3,2,1,0:T(2,128)} reshape(f32[8,10240]{1,0:T(8,128)S(1)} %reduce) | data formatting | bytes 655360
  414.7 10.3 %copy.55 = f32[5,2,2,8,512]{4,2,3,1,0:T(2,128)S(1)} copy(f32[5,2,2,8,512]{0,2,1,4,3:T(2,128)} %bitcast.159) | data formatting | bytes 655360 | tf_op jit(solution)/shard_map/all_to_all | solution.py:126
  427.3 90.3 %all-gather.3.cloned.1.call-done = f32[64,2,16,512]{3,2,1,0:T(8,128)} async-done(((f32[1,2,16,512]{3,2,1,0:T(8,128)}), f32[64,2,16,512]{3,2,1,0:T(8,128)}) %all-gather.3.cloned.1.call-update) | async-done | bytes 4194320 | tf_op jit(solution)/shard_map/all_gather | solution.py:38
  517.6 85.3 %all-gather.5.cloned.1.call-done = f32[64,2,16,512]{3,2,1,0:T(8,128)} async-done(((f32[1,2,16,512]{3,2,1,0:T(8,128)}), f32[64,2,16,512]{3,2,1,0:T(8,128)}) %all-gather.5.cloned.1.call-update) | async-done | bytes 4194320 | tf_op jit(solution)/shard_map/all_gather | solution.py:38
  603.0 59.0 %while.14 = (s32[]{:T(128)}, f32[2,16,512]{2,1,0:T(8,128)S(1)}, s32[]{:T(128)}, f32[64,2,16,512]{3,2,1,0:T(8,128)}, f32[64,2,16,512]{3,2,1,0:T(8,128)}, /*index=5*/s32[]{:T(128)}, s32[]{:T(128)}) while((s32[]{:T(128)}, f32[2,16,512]{2,1,0:T(8,128)S(1)}, s32[]{:T(128)}, f32[64,2,16,512]{3,2,1,0:T(8,128)}, ...), condition=%wide.region_2.3_spmd.clone, body=%wide.region_1.2_spmd.clone.sunk | while | flops 65540 | bytes 262245 | solution.py:47
  608.6 0.9 fusion.117
  617.0 0.9 fusion.117
  663.5 6.5 all-to-all-start.1
  669.9 11.9 %all-to-all-done.1 = f32[2,2,32,512]{3,1,0,2:T(2,128)S(1)} async-done(((f32[2,2,32,512]{3,1,0,2:T(2,128)}), f32[2,2,32,512]{3,1,0,2:T(2,128)S(1)}, u32[]{:S(2)}, u32[]{:S(2)}) %all-to-all-start.1) | async-done | bytes 262176 | tf_op jit(solution)/shard_map/all_to_all | solution.py:162
  682.9 1.9 convolution_bitcast_fusion
  685.0 1.3 copy.58
  (116 shorter events, 67.7 us)
Async XLA Ops:
  6.5 6.1 copy-start.4
  8.1 10.6 %collective-permute-start = (f32[2,4,128,128]{2,3,1,0:T(8,128)S(1)}, f32[2,4,128,128]{2,3,1,0:T(8,128)S(1)}, u32[]{:S(2)}, u32[]{:S(2)}) collective-permute-start(f32[2,4,128,128]{2,3,1,0:T(8,128)S(1)} %bitcast.168), channel_id=1, source_target_pairs={{0,8},{8,16},{16,24},{24,32},{32,40},{40,48},{48,56},{56,64},{64,7... | collective-permute-start | bytes 1572872 | tf_op jit(solution)/shard_map/ppermute | solution.py:33
  18.9 12.3 %collective-permute-start.1 = (f32[3,2,1,128,128]{3,4,2,1,0:T(8,128)S(1)}, f32[3,2,1,128,128]{3,4,2,1,0:T(8,128)S(1)}, u32[]{:S(2)}, u32[]{:S(2)}) collective-permute-start(f32[3,2,1,128,128]{3,4,2,1,0:T(8,128)S(1)} %get-tuple-element.136), channel_id=1, source_target_pairs={{1,0},{2,1},{3,2},{4,3},{5,4},{6,5},{7,6},{9,8},{10,9},{11,10},{12... | collective-permute-start | bytes 1179656 | tf_op jit(solution)/shard_map/ppermute | solution.py:25
  20.2 12.8 %collective-permute-start.2 = (f32[3,2,1,128,128]{3,4,2,1,0:T(8,128)S(1)}, f32[3,2,1,128,128]{3,4,2,1,0:T(8,128)S(1)}, u32[]{:S(2)}, u32[]{:S(2)}) collective-permute-start(f32[3,2,1,128,128]{3,4,2,1,0:T(8,128)S(1)} %get-tuple-element.137), channel_id=1, source_target_pairs={{0,1},{1,2},{2,3},{3,4},{4,5},{5,6},{6,7},{8,9},{9,10},{10,11},{11... | collective-permute-start | bytes 1179656 | tf_op jit(solution)/shard_map/ppermute | solution.py:24
  34.5 7.4 %collective-permute-start.3 = (f32[1,2,1,128,128]{3,4,2,1,0:T(8,128)S(1)}, f32[1,2,1,128,128]{3,4,2,1,0:T(8,128)S(1)}, u32[]{:S(2)}, u32[]{:S(2)}) collective-permute-start(f32[1,2,1,128,128]{3,4,2,1,0:T(8,128)S(1)} %get-tuple-element.148), channel_id=1, source_target_pairs={{1,0},{2,1},{3,2},{4,3},{5,4},{6,5},{7,6},{9,8},{10,9},{11,10},{12... | collective-permute-start | bytes 393224 | tf_op jit(solution)/shard_map/ppermute | solution.py:25
  35.8 7.0 %collective-permute-start.4 = (f32[1,2,1,128,128]{3,4,2,1,0:T(8,128)S(1)}, f32[1,2,1,128,128]{3,4,2,1,0:T(8,128)S(1)}, u32[]{:S(2)}, u32[]{:S(2)}) collective-permute-start(f32[1,2,1,128,128]{3,4,2,1,0:T(8,128)S(1)} %get-tuple-element.149), channel_id=1, source_target_pairs={{0,1},{1,2},{2,3},{3,4},{4,5},{5,6},{6,7},{8,9},{9,10},{10,11},{11... | collective-permute-start | bytes 393224 | tf_op jit(solution)/shard_map/ppermute | solution.py:24
  43.2 0.7 copy-start.2
  44.6 181.6 %collective-permute-start.5 = (f32[1,2,1,128,128]{3,4,2,1,0:T(8,128)}, f32[1,2,1,128,128]{3,4,2,1,0:T(8,128)S(1)}, u32[]{:S(2)}, u32[]{:S(2)}) collective-permute-start(f32[1,2,1,128,128]{3,4,2,1,0:T(8,128)} %get-tuple-element.146), channel_id=1, source_target_pairs={{1,0},{2,1},{3,2},{4,3},{5,4},{6,5},{7,6},{9,8},{10,9},{11,10},{12... | collective-permute-start | bytes 393224 | tf_op jit(solution)/shard_map/ppermute | solution.py:25
  45.9 180.3 %collective-permute-start.6 = (f32[1,2,1,128,128]{3,4,2,1,0:T(8,128)}, f32[1,2,1,128,128]{3,4,2,1,0:T(8,128)}, u32[]{:S(2)}, u32[]{:S(2)}) collective-permute-start(f32[1,2,1,128,128]{3,4,2,1,0:T(8,128)} %get-tuple-element.147), channel_id=1, source_target_pairs={{0,1},{1,2},{2,3},{3,4},{4,5},{5,6},{6,7},{8,9},{9,10},{10,11},{11... | collective-permute-start | bytes 393224 | tf_op jit(solution)/shard_map/ppermute | solution.py:24
  226.3 1.4 copy-start.3
  348.1 1.6 copy-start
  349.7 1.6 copy-start.1
  381.1 15.3 %all-to-all-start = ((f32[8,1,10240]{2,1,0:T(1,128)}), f32[8,1,10240]{2,1,0:T(1,128)S(1)}, u32[]{:S(2)}, u32[]{:S(2)}) async-start(f32[8,1,10240]{2,1,0:T(1,128)} %reshape.463), calls=%async_computation | async-start | bytes 655360 | tf_op jit(solution)/shard_map/all_to_all | solution.py:126
  385.5 132.1 %all-gather.3.cloned.1.call-start = ((), (), s32[]{:S(2)}) async-start(), calls=%async_computation.2 | async-start | bytes 4259840 | tf_op jit(solution)/shard_map/all_gather | solution.py:38
  426.5 176.4 %all-gather.5.cloned.1.call-start = ((), (), s32[]{:S(2)}) async-start(), calls=%async_computation.3 | async-start | bytes 4259840 | tf_op jit(solution)/shard_map/all_gather | solution.py:38
  663.5 18.4 %all-to-all-start.1 = ((f32[2,2,32,512]{3,1,0,2:T(2,128)}), f32[2,2,32,512]{3,1,0,2:T(2,128)S(1)}, u32[]{:S(2)}, u32[]{:S(2)}) async-start(f32[2,2,32,512]{3,1,0,2:T(2,128)} %copy.56), calls=%async_computation.1 | async-start | bytes 524288 | tf_op jit(solution)/shard_map/all_to_all | solution.py:162
Sparse Core Ops, SparseCore 0:
  426.6 90.9 all-gather.2
  521.0 81.9 all-gather.4
where the time goes:
time: 699 us; the launch traced here: 693 us
  local copies, waits for them, and re-layouts  354 us (51%)
  waiting for transfers between devices  216 us (31%)
  other arithmetic  68.3 us (10%)
  starting transfers between devices  33.2 us (5%)
  between operations  13.8 us (2%)
    another operation x11, local copies, waits for them, and re-layouts, local(): jnp.stack([integral_one, integral_two, start_value, swept_one, swept_two])  293 us
    all_gather x2, waiting for transfers between devices, entering(): pieces = jax.tree.map(lambda part: lax.all_gather(part, axis), value)  176 us
    select_n x63, other arithmetic, lap(): jnp.where(position < mine, new, old)  57.7 us
    unnamed x19, local copies, waits for them, and re-layouts  36 us
  transfers between devices with their start and end apart: 11, of which 9 were waited for; matrix products, arithmetic and copies ran while one was open for 25% of the time, Pallas kernels for 0%

commit v1 on v0

v1 whole, which is shorter than its diff:
```python
import functools
import math

import jax
import jax.numpy as jnp
import ml_dtypes
import numpy as np
from jax import lax
from jax.experimental import pallas as pl
from jax.experimental.pallas import tpu as pltpu
from jax.sharding import PartitionSpec as P

MESH = pl.DeviceIdType.MESH
DIFFUSE = (0.5, 0.25)
DECAY = (0.04, 0.1)
SIGN = (-1.0, 1.0)
DT = 0.5
H = 0.25
S = ((5.0 / 24.0, 1.0 / 3.0, -1.0 / 24.0), (-1.0 / 24.0, 1.0 / 3.0, 5.0 / 24.0))
ROWS = 32


def sine_table(points, modes, stretch):
    place = np.arange(points) + 0.5
    order = np.arange(modes) + 1.0
    angle = math.pi / (stretch * modes) * place[:, None] * order[None, :]
    weight = np.where(np.arange(modes) == modes - 1, math.sqrt(0.5), 1.0)
    return math.sqrt(2.0 / modes) * weight[None, :] * np.sin(angle)


def two_parts(table):
    high = table.astype(np.float32).astype(ml_dtypes.bfloat16)
    low = (table - high.astype(np.float64)).astype(np.float32).astype(ml_dtypes.bfloat16)
    return np.stack([high, low])


@functools.lru_cache(maxsize=None)
def tables(n, spaces):
    m, mz = n // 2, 2 * spaces
    half = m // 2
    per = half // spaces
    average = np.kron(np.eye(m), np.array([[0.5, 0.5]]))
    fine = sine_table(m, m, 1.0).T @ average
    fx = np.zeros((2, half, 2, 2, n))
    for z in range(2):
        fx[:, :, z, z, :] = 0.5 * fine.reshape(2, half, n)
    fx = fx.reshape(2 * m, 2 * n)
    fy = np.kron(np.eye(2), fine.T)
    wz = sine_table(mz, mz, 1.0).T
    own = np.zeros((mz, per, spaces, per, 2))
    edge = np.zeros((mz, per, spaces, per, 2))
    for i in range(per):
        for y in range(spaces):
            for z in range(2):
                own[:, i, y, i, z] = wz[:, 2 * y + z]
            if y > 0:
                edge[:, i, y, i, 0] = wz[:, 2 * y - 1]
            if y < spaces - 1:
                edge[:, i, y, i, 1] = wz[:, 2 * y + 2]
    own, edge = own.reshape(m, m), edge.reshape(m, m)
    mats = np.stack(
        [np.concatenate([own, edge * (DT * S[i][2])], axis=1) for i in range(2)]
    )
    nz = np.kron(sine_table(2 * mz, mz, 2.0), np.eye(per))
    vxy = sine_table(n, m, 2.0)
    vy = np.kron(np.eye(2), vxy.T)
    vx = np.zeros((4, n, 2, spaces, 4, per))
    for f in range(4):
        vx[f, :, :, :, f, :] = vxy.reshape(n, 2, spaces, per)
    vx = vx.reshape(4 * n, 2 * spaces * 4 * per)

    def eigen(modes):
        return 2.0 * np.cos(math.pi * (np.arange(modes) + 1.0) / modes) - 2.0

    ab = (eigen(m)[:, None] + eigen(m)[None, :]).reshape(2, spaces, per, m)
    e = (eigen(mz)[None, :, None, None, None] + ab.transpose(1, 2, 0, 3)[:, None]) / 4.0
    lin = np.stack([d * e - k for d, k in zip(DIFFUSE, DECAY)])
    factor = 1.0 / (1.0 - H * lin)
    factor = factor.reshape(2, spaces, m, n).astype(np.float32)
    return tuple(map(two_parts, (fx, fy, mats[0], mats[1], nz, vy, vx))) + (factor,)


def split(x):
    high = x.astype(jnp.bfloat16)
    low = (x - high.astype(jnp.float32)).astype(jnp.bfloat16)
    return high, low


def dot(a, b):
    return jnp.dot(a, b, preferred_element_type=jnp.float32)


def left(table, x):
    high, low = split(x)
    return dot(table[0], high) + (dot(table[0], low) + dot(table[1], high))


def right(x, table):
    high, low = split(x)
    return dot(high, table[0]) + (dot(low, table[0]) + dot(high, table[1]))


def kernel(
    shape,
    nodes, initial, fx_h, fy_h, m0_h, m1_h, nz_h, vy_h, vx_h, p_h,
    out,
    u, s1, s2, a, g, fx, fy, m0, m1, nz, vy, vx, pw,
    spec, c2in, gather, e2, xin, tot, zin, back, pre, fine, fin,
    ssem, lsem, r_u0, r_h, r_u0h, r_s1, r_c2, r_in, r_x, r_z, r_b, r_f,
):
    count, spaces, chips_x, chips_z, n = shape
    tm, sp = lax.axis_index("tm"), lax.axis_index("space")
    core = lax.rem(tm, 2)
    chip = tm // 2
    cx, cz = lax.rem(chip, chips_x), chip // chips_x
    sends = []

    def at(z, x, c):
        return (z * chips_x + x) * 2 + c

    def send(src, dst, sem, device, when=None):
        copy = pltpu.make_async_remote_copy(
            src, dst, ssem.at[len(sends)], sem, device_id=device, device_id_type=MESH
        )
        sends.append((copy, when))
        if when is None:
            copy.start()
        else:
            pl.when(when)(copy.start)

    def arrived(dst, sem):
        pltpu.make_async_copy(dst, dst, sem).wait()

    has_lo, has_hi = sp > 0, sp < spaces - 1
    lo, hi = (tm, jnp.maximum(sp - 1, 0)), (tm, jnp.minimum(sp + 1, spaces - 1))
    has_next, has_prior = tm < count - 1, tm > 0
    nxt = (lax.rem(tm + 1, count), sp)
    prv = (lax.rem(tm + count - 1, count), sp)
    yc = [(d % spaces, d // spaces) for d in range(1, 2 * spaces)]

    def owner(d):
        return lax.rem(sp + d[0], spaces), lax.rem(core + d[1], 2)

    x_peers = [lax.rem(cx + d, chips_x) for d in range(1, chips_x)]
    z_peers = [lax.rem(cz + d, chips_z) for d in range(1, chips_z)]

    loads = [
        pltpu.make_async_copy(nodes.at[0, 0], u.at[1, :, pl.ds(1, 4)], lsem.at[0]),
        pltpu.make_async_copy(nodes.at[0, 1], u.at[2, :, pl.ds(1, 4)], lsem.at[1]),
        pltpu.make_async_copy(fx_h, fx, lsem.at[2]),
        pltpu.make_async_copy(fy_h, fy, lsem.at[3]),
        pltpu.make_async_copy(m0_h, m0, lsem.at[4]),
        pltpu.make_async_copy(m1_h, m1, lsem.at[5]),
        pltpu.make_async_copy(nz_h, nz, lsem.at[6]),
        pltpu.make_async_copy(vy_h, vy, lsem.at[7]),
        pltpu.make_async_copy(vx_h, vx, lsem.at[8]),
        pltpu.make_async_copy(p_h.at[core, sp], pw, lsem.at[9]),
    ]
    for load in loads:
        load.start()
    pieces = [(0, 1), (3, 1), (1, 2)]

    @pl.when(tm == 0)
    def _():
        for i, (z, length) in enumerate(pieces):
            pltpu.make_async_copy(
                initial.at[:, pl.ds(z, length)], u.at[0, :, pl.ds(1 + z, length)], r_u0.at[i]
            ).start()

    barrier = pltpu.get_barrier_semaphore()
    peers = []
    for d in yc:
        y, c = owner(d)
        peers.append((chip * 2 + c, y))
    peers += [(at(cz, x, core), sp) for x in x_peers]
    peers += [(at(z, cx, core), sp) for z in z_peers]
    peers.append((lax.rem(tm + count - 1 + 2 * core, count), sp))
    for peer in peers:
        pl.semaphore_signal(barrier, 1, device_id=peer, device_id_type=MESH)
    pl.semaphore_wait(barrier, len(peers))

    for node in (2, 1):
        send(nodes.at[0, node - 1, :, 3], u.at[node, :, 0], r_h.at[node - 1, 0], hi, has_hi)
        send(nodes.at[0, node - 1, :, 0], u.at[node, :, 5], r_h.at[node - 1, 1], lo, has_lo)
    for i, (z, length) in enumerate(pieces):
        send(
            nodes.at[0, 1, :, pl.ds(z, length)], u.at[0, :, pl.ds(1 + z, length)],
            r_u0.at[i], nxt, has_next,
        )

    zero = jnp.zeros((n, n), jnp.float32)
    for s in range(2):
        for z in range(6):
            a[s, z, 0:8, :] = jnp.zeros((8, n), jnp.float32)
            a[s, z, 8 + n : 16 + n, :] = jnp.zeros((8, n), jnp.float32)

    def outside(plane):
        for s in range(2):
            for i in range(3):
                u[i, s, plane] = zero
            s1[s, plane] = zero

    pl.when(sp == 0)(lambda: outside(0))
    pl.when(sp == spaces - 1)(lambda: outside(5))

    @pl.when(tm == 0)
    def _():
        c2in[...] = jnp.zeros(c2in.shape, jnp.float32)

    lane = lax.broadcasted_iota(jnp.int32, (ROWS, n), 1)
    first_lane, last_lane = lane == 0, lane == n - 1
    chunks = range(0, n, ROWS)

    def react(p, q):
        return (1.0 + p) * (q * q)

    def sides(s, z, r):
        mid = a[s, z, 8 + r : 8 + r + ROWS, :]
        west = jnp.where(first_lane, 0.0, pltpu.roll(mid, 1, 1))
        east = jnp.where(last_lane, 0.0, pltpu.roll(mid, n - 1, 1))
        north = a[s, z, 7 + r : 7 + r + ROWS, :]
        south = a[s, z, 9 + r : 9 + r + ROWS, :]
        return (west + east) + (north + south), mid

    def rows(ref, *index, r):
        return ref[(*index, slice(r, r + ROWS), slice(None))]

    def sum_one(z, base=True):
        for r in chunks:
            pq = [[rows(u, i, s, z, r=r) for s in range(2)] for i in range(3)]
            if base:
                w = sum((DT * S[0][i]) * react(*pq[i]) for i in range(3))
            for s in range(2):
                total = sum((DT * S[0][i]) * pq[i][s] for i in range(3))
                a[s, z, 8 + r : 8 + r + ROWS, :] = total
                if base:
                    s1[s, z, r : r + ROWS, :] = pq[0][s] + SIGN[s] * w - DECAY[s] * total

    def sum_two(z, base=True):
        weight = (DT * S[1][0], DT * S[1][1] - H, DT * S[1][2])
        for r in chunks:
            pq = [[rows(u, i, s, z, r=r) for s in range(2)] for i in range(3)]
            ab = [rows(s1, s, z, r=r) for s in range(2)]
            if base:
                w = H * react(*ab) + sum(weight[i] * react(*pq[i]) for i in range(3))
            for s in range(2):
                total = H * ab[s] + sum(weight[i] * pq[i][s] for i in range(3))
                a[s, z, 8 + r : 8 + r + ROWS, :] = total
                if base:
                    s2[s, z - 1, r : r + ROWS, :] = ab[s] + SIGN[s] * w - DECAY[s] * total

    def diffuse(ref, z, shift):
        for r in chunks:
            for s in range(2):
                around, mid = sides(s, z, r)
                below = a[s, z - 1, 8 + r : 8 + r + ROWS, :]
                above = a[s, z + 1, 8 + r : 8 + r + ROWS, :]
                lap = around + (below + above) - 6.0 * mid
                ref[s, z - shift, r : r + ROWS, :] = (
                    ref[s, z - shift, r : r + ROWS, :] + DIFFUSE[s] * lap
                )

    loads[0].wait()
    loads[1].wait()
    even = core == 0
    arrived(u.at[0, :, pl.ds(1, 1)], r_u0.at[0])
    arrived(u.at[0, :, pl.ds(4, 1)], r_u0.at[1])
    send(u.at[0, :, 4], u.at[0, :, 0], r_u0h.at[0], hi, has_hi & even)
    send(u.at[0, :, 1], u.at[0, :, 5], r_u0h.at[1], lo, has_lo & even)
    pl.when(has_lo)(lambda: arrived(u.at[2, :, 0], r_h.at[1, 0]))
    pl.when(has_hi)(lambda: arrived(u.at[2, :, 5], r_h.at[1, 1]))
    send(u.at[2, :, 0], u.at[0, :, 0], r_u0h.at[0], nxt, has_lo & even)
    send(u.at[2, :, 5], u.at[0, :, 5], r_u0h.at[1], nxt, has_hi & even)
    arrived(u.at[0, :, pl.ds(2, 2)], r_u0.at[2])
    for z in (1, 2, 3, 4):
        sum_one(z)
    for z in (2, 3):
        diffuse(s1, z, 0)
    pl.when(has_lo)(lambda: arrived(u.at[1, :, 0], r_h.at[0, 0]))
    pl.when(has_lo)(lambda: arrived(u.at[0, :, 0], r_u0h.at[0]))
    sum_one(0, False)
    diffuse(s1, 1, 0)
    send(s1.at[:, 1], s1.at[:, 5], r_s1.at[1], lo, has_lo)
    pl.when(has_hi)(lambda: arrived(u.at[1, :, 5], r_h.at[0, 1]))
    pl.when(has_hi)(lambda: arrived(u.at[0, :, 5], r_u0h.at[1]))
    sum_one(5, False)
    diffuse(s1, 4, 0)
    send(s1.at[:, 4], s1.at[:, 0], r_s1.at[0], hi, has_hi)

    for z in (1, 2, 3, 4):
        sum_two(z)
    for z in (2, 3):
        diffuse(s2, z, 1)
    pl.when(has_lo)(lambda: arrived(s1.at[:, 0], r_s1.at[0]))
    pl.when(has_hi)(lambda: arrived(s1.at[:, 5], r_s1.at[1]))
    sum_two(0, False)
    sum_two(5, False)
    diffuse(s2, 1, 1)
    diffuse(s2, 4, 1)

    is_first = jnp.where(tm == 0, 1.0, 0.0)
    for i in range(2):
        for j in range(2):
            z = 2 * j + 1
            for r in chunks:
                w = 0.0
                both = [0.0, 0.0]
                keep = [0.0, 0.0]
                for k in (z, z + 1):
                    p0 = [rows(u, 0, s, k, r=r) for s in range(2)]
                    p1 = [rows(s1, s, k, r=r) for s in range(2)]
                    p2 = [rows(s2, s, k - 1, r=r) for s in range(2)]
                    three = (p0, p1, p2)
                    w = w + sum((DT * S[i][t]) * react(*three[t]) for t in range(3))
                    for s in range(2):
                        total = sum((DT * S[i][t]) * three[t][s] for t in range(3))
                        both[s] = both[s] + total
                        if i == 0:
                            keep[s] = keep[s] + is_first * p0[s] - p1[s]
                        else:
                            keep[s] = keep[s] + p1[s] - p2[s]
                for s in range(2):
                    out_of = 0 if j == 0 else 5
                    near = 3 if j == 0 else 2
                    beyond = (DT * S[i][0]) * rows(u, 0, s, out_of, r=r) + (DT * S[i][1]) * rows(
                        s1, s, out_of, r=r
                    )
                    beyond = beyond + (
                        (DT * S[i][0]) * rows(u, 0, s, near, r=r)
                        + (DT * S[i][1]) * rows(s1, s, near, r=r)
                        + (DT * S[i][2]) * rows(s2, s, near - 1, r=r)
                    )
                    a[s, j, 8 + r : 8 + r + ROWS, :] = both[s]
                    g[i, j, r : r + ROWS, s * n : (s + 1) * n] = (
                        keep[s]
                        + SIGN[s] * w
                        - DECAY[s] * both[s]
                        + DIFFUSE[s] * (beyond - 5.0 * both[s])
                    )
            for r in chunks:
                for s in range(2):
                    around, _ = sides(s, j, r)
                    at_s = slice(s * n, (s + 1) * n)
                    g[i, j, r : r + ROWS, at_s] = (
                        g[i, j, r : r + ROWS, at_s] + DIFFUSE[s] * around
                    )
    for j in range(2):
        for r in chunks:
            for s in range(2):
                at_s = slice(s * n, (s + 1) * n)
                g[2, j, r : r + ROWS, at_s] = DIFFUSE[s] * rows(s2, s, 3 * j, r=r)
                g[3, j, r : r + ROWS, at_s] = rows(s2, s, 2 * j, r=r) + rows(s2, s, 2 * j + 1, r=r)

    for load in loads[2:]:
        load.wait()

    def to_modes(i):
        both = jnp.concatenate([g[i, 0], g[i, 1]], axis=0)
        along_x = left(fx, both)
        for s in range(2):
            at_s = slice(s * n, (s + 1) * n)
            wide = jnp.concatenate([along_x[: n // 2, at_s], along_x[n // 2 :, at_s]], axis=1)
            spec[s, i] = right(wide, fy)

    part = n // 2 // spaces
    to_modes(3)
    send(spec.at[:, 3], c2in, r_c2, nxt, has_next)
    for i in (1, 2, 0):
        to_modes(i)
    pl.when(has_prior)(lambda: arrived(c2in, r_c2))
    for s in range(2):
        spec[s, 0] = spec[s, 0] + c2in[s]

    def mine(y):
        return pl.ds(pl.multiple_of(y * part, part), part)

    for d in yc:
        y, c = owner(d)
        send(spec.at[c, pl.ds(0, 3), mine(y)], gather.at[core, :, sp], r_in.at[core, sp], (chip * 2 + c, y))
    gather[core, :, sp] = spec[core, 0:3, mine(sp)]
    for d in yc:
        y, c = owner(d)
        arrived(gather.at[c, :, y], r_in.at[c, y])

    m = n // 2
    power = pw[...]
    square = power * power
    d0, d1 = [], []
    for c in range(2):
        own = [gather[c, i].reshape(m, n) for i in range(3)]
        d0.append(left(m0, jnp.concatenate([own[0], own[2]], axis=0)))
        d1.append(left(m1, jnp.concatenate([own[1], own[2]], axis=0)))
    e = [power * (power * d0[c] + d1[c]) for c in range(2)]
    e2[...] = square * e[0] + e[1]

    share = m // chips_x

    def shared(x):
        return pl.ds(pl.multiple_of(x * share, share), share)

    for x in x_peers:
        send(e2.at[shared(x)], xin.at[cx], r_x.at[cx], (at(cz, x, core), sp))
    xin[cx] = e2[shared(cx)]
    for x in x_peers:
        arrived(xin.at[x], r_x.at[x])
    p1 = pw[shared(cx)]
    p2 = p1 * p1
    p4 = p2 * p2
    running = jnp.zeros((share, n), jnp.float32)
    before, ahead = [], []
    power_x = jnp.ones((share, n), jnp.float32)
    for x in range(chips_x):
        before.append(running)
        ahead.append(power_x)
        running = p4 * running + xin[x]
        power_x = power_x * p4
    tot[...] = running
    for z in z_peers:
        send(tot, zin.at[cz], r_z.at[cz], (at(z, cx, core), sp))
    zin[cz] = running
    for z in z_peers:
        arrived(zin.at[z], r_z.at[z])
    earlier = jnp.zeros((share, n), jnp.float32)
    for z in range(chips_z):
        earlier = jnp.where(z < cz, power_x * earlier + zin[z], earlier)
    for x in range(chips_x):
        back[x] = ahead[x] * earlier + before[x]
    for x in x_peers:
        send(back.at[x], pre.at[shared(cx)], r_b.at[cx], (at(cz, x, core), sp))
    pre[shared(cx)] = back[cx]
    for x in x_peers:
        arrived(pre.at[shared(x)], r_b.at[x])

    change = pre[...]
    for c in range(2):
        for f, source in enumerate((d0[c], d1[c])):
            change = power * (change + source)
            fine[c, f] = left(nz, change)
    rows_back = 2 * part

    def planes(y):
        return pl.ds(pl.multiple_of(y * rows_back, rows_back), rows_back)

    for d in yc:
        y, c = owner(d)
        send(fine.at[c, :, planes(y)], fin.at[:, core, sp], r_f.at[core, sp], (chip * 2 + c, y))
    fin[:, core, sp] = fine[core, :, planes(sp)]
    for d in yc:
        y, c = owner(d)
        arrived(fin.at[:, c, y], r_f.at[c, y])

    for f in range(2):
        tall = []
        for s in range(2):
            wide = right(fin[f, s].reshape(n, n), vy)
            tall.append(jnp.concatenate([wide[:, :n], wide[:, n:]], axis=0))
        refined = left(vx, jnp.concatenate(tall, axis=1))
        for s in range(2):
            for z in range(4):
                piece = refined[z * n : (z + 1) * n, s * n : (s + 1) * n]
                swept = s1[s, z + 1] if f == 0 else s2[s, z]
                out[0, f, s, z] = swept + piece

    for copy, when in sends:
        if when is None:
            copy.wait_send()
        else:
            pl.when(when)(copy.wait_send)


def local(shape, nodes, initial):
    count, spaces, chips_x, chips_z, n = shape
    consts = tables(n, spaces)
    m = n // 2
    part = m // spaces
    share = m // chips_x
    f32 = jnp.float32
    vmem, sem = pltpu.VMEM, pltpu.SemaphoreType.DMA
    n_sends = 4 + 3 + 4 + 2 + 1 + 2 * (2 * spaces - 1) + 2 * (chips_x - 1) + chips_z - 1
    scratch = [
        vmem((3, 2, 6, n, n), f32),
        vmem((2, 6, n, n), f32),
        vmem((2, 4, n, n), f32),
        vmem((2, 6, n + 16, n), f32),
        vmem((4, 2, n, 2 * n), f32),
    ]
    scratch += [vmem(c.shape, jnp.bfloat16) for c in consts[:-1]]
    scratch += [
        vmem((m, n), f32),
        vmem((2, 4, m, n), f32),
        vmem((2, m, n), f32),
        vmem((2, 3, spaces, part, n), f32),
        vmem((m, n), f32),
        vmem((chips_x, share, n), f32),
        vmem((share, n), f32),
        vmem((chips_z, share, n), f32),
        vmem((chips_x, share, n), f32),
        vmem((m, n), f32),
        vmem((2, 2, n, n), f32),
        vmem((2, 2, spaces, 2 * part, n), f32),
        sem((n_sends,)),
        sem((10,)),
        sem((3,)),
        sem((2, 2)),
        sem((2,)),
        sem((2,)),
        sem(()),
        sem((2, spaces)),
        sem((chips_x,)),
        sem((chips_z,)),
        sem((chips_x,)),
        sem((2, spaces)),
    ]
    anywhere = pl.BlockSpec(memory_space=pl.ANY)
    return pl.pallas_call(
        functools.partial(kernel, shape),
        out_shape=jax.ShapeDtypeStruct((1, 2, 2, 4, n, n), f32),
        in_specs=[anywhere] * (2 + len(consts)),
        out_specs=pl.BlockSpec(memory_space=pltpu.VMEM),
        scratch_shapes=scratch,
        compiler_params=pltpu.CompilerParams(
            collective_id=0, has_side_effects=True, vmem_limit_bytes=48 << 20
        ),
        name="iteration",
    )(nodes, initial, *[jnp.asarray(c) for c in consts])


def solution(mesh):
    count, spaces = mesh.shape["tm"], mesh.shape["space"]
    chips_x = 4 if count == 64 else 2
    chips_z = count // (2 * chips_x)
    in_specs = (P("tm", None, None, "space", None, None), P(None, "space", None, None))
    out_specs = P("tm", None, None, "space", None, None)

    def run(nodes, initial):
        shape = (count, spaces, chips_x, chips_z, nodes.shape[-1])
        return jax.shard_map(
            functools.partial(local, shape),
            mesh=mesh, in_specs=in_specs, out_specs=out_specs, check_vma=False,
        )(nodes, initial)

    return run
```

time: 699 us -> 72.9 us (0.10)
  local copies, waits for them, and re-layouts: 354 us -> 10.4 us
  waiting for transfers between devices: 216 us -> 0 us
  other arithmetic: 68.3 us -> 0 us
  Pallas kernels: 0 us -> 62 us
  starting transfers between devices: 33.2 us -> 0 us
  between operations: 13.8 us -> 0.02 us
    another operation x11 -> x0, local copies, waits for them, and re-layouts: 293 us -> none  [local(): jnp.stack([integral_one, integral_two, start_value, swept_one, swept_two])]
    all_gather x2 -> x0, waiting for transfers between devices: 176 us -> none  [entering(): pieces = jax.tree.map(lambda part: lax.all_gather(part, axis), value)]
    pallas_call x0 -> x1, Pallas kernels: none -> 62 us  [local(): pl.pallas_call(functools.partial(kernel, shape), out_shape=jax.ShapeDtype...]
    select_n x64 -> x0, other arithmetic: 57.7 us -> none  [the longest x63 57.7 us: lap(): jnp.where(position < mine, new, old)]
    unnamed x19 -> x21, local copies, waits for them, and re-layouts: 36 us -> 10.4 us
    all_to_all x2 -> x0, waiting for transfers between devices: 22.5 us -> none  [the longest x1 11.9 us: local(): lax.all_to_all(at_planes, 'space', split_axis=2, concat_axis=3, tiled=True)]
    ppermute x7 -> x0, starting transfers between devices: 22.3 us -> none  [the longest x3 13.9 us: with_halo(): before = lax.ppermute(last, axis, up)]
    ppermute x7 -> x0, waiting for transfers between devices: 16.9 us -> none  [the longest x3 8.55 us: with_halo(): after = lax.ppermute(leading, axis, down)]
  transfers between devices with their start and end apart: 11 -> 0, of which waited for: 9 -> 0; matrix products, arithmetic and copies ran while one was open for 25% -> 0% of each run, Pallas kernels for 0% -> 0%
where the time goes in v1:
time: 72.9 us; the launch traced here: 72.4 us
  Pallas kernels  62 us (85%)
  local copies, waits for them, and re-layouts  10.4 us (14%)
    pallas_call x1, Pallas kernels, local(): pl.pallas_call(functools.partial(kernel, shape), out_shape=jax.ShapeDtype...  62 us
    unnamed x21, local copies, waits for them, and re-layouts  10.4 us

profile of v1, /device:TPU:1, one launch (start us, length us, event | category | flops | bytes accessed | tf_op | source)
XLA Modules:
  0.0 72.4 jit_solution(12955412118292564244)
XLA Ops:
  0.0 0.0 copy-start
  0.0 1.2 %copy-done = f32[1,2,2,4,128,128]{5,4,3,2,1,0:T(8,128)S(1)} copy-done((f32[1,2,2,4,128,128]{5,4,3,2,1,0:T(8,128)S(1)}, f32[1,2,2,4,128,128]{5,4,3,2,1,0:T(8,128)}, u32[]{:S(2)}) %copy-start) | copy-done | bytes 1048600
  1.2 0.0 copy-start.1
  1.2 1.0 %copy-done.1 = f32[2,4,128,128]{3,2,1,0:T(8,128)S(1)} copy-done((f32[2,4,128,128]{3,2,1,0:T(8,128)S(1)}, f32[2,4,128,128]{3,2,1,0:T(8,128)}, u32[]{:S(2)}) %copy-start.1) | copy-done | bytes 524312
  2.3 0.0 copy-start.2
  2.3 1.0 %copy-done.2 = f32[2,8,64,128]{3,2,1,0:T(8,128)S(1)} copy-done((f32[2,8,64,128]{3,2,1,0:T(8,128)S(1)}, f32[2,8,64,128]{3,2,1,0:T(8,128)}, u32[]{:S(2)}) %copy-start.2) | copy-done | bytes 524312
  3.3 0.0 copy-start.3
  3.3 1.0 %copy-done.3 = bf16[2,512,256]{2,1,0:T(8,128)(2,1)S(1)} copy-done((bf16[2,512,256]{2,1,0:T(8,128)(2,1)S(1)}, bf16[2,512,256]{2,1,0:T(8,128)(2,1)}, u32[]{:S(2)}) %copy-start.3) | copy-done | bytes 524312
  4.4 0.0 copy-start.4
  4.4 0.9 %copy-done.4 = bf16[2,128,256]{2,1,0:T(8,128)(2,1)S(1)} copy-done((bf16[2,128,256]{2,1,0:T(8,128)(2,1)S(1)}, bf16[2,128,256]{2,1,0:T(8,128)(2,1)}, u32[]{:S(2)}) %copy-start.4) | copy-done | bytes 131096
  5.3 0.0 copy-start.5
  5.3 0.9 %copy-done.5 = bf16[2,256,128]{2,1,0:T(8,128)(2,1)S(1)} copy-done((bf16[2,256,128]{2,1,0:T(8,128)(2,1)S(1)}, bf16[2,256,128]{2,1,0:T(8,128)(2,1)}, u32[]{:S(2)}) %copy-start.5) | copy-done | bytes 131096
  6.2 0.0 copy-start.6
  6.2 0.9 %copy-done.6 = bf16[2,128,256]{2,1,0:T(8,128)(2,1)S(1)} copy-done((bf16[2,128,256]{2,1,0:T(8,128)(2,1)S(1)}, bf16[2,128,256]{2,1,0:T(8,128)(2,1)}, u32[]{:S(2)}) %copy-start.6) | copy-done | bytes 131096
  7.1 0.0 copy-start.7
  7.1 0.8 %copy-done.7 = bf16[2,128,64]{2,1,0:T(8,128)(2,1)S(1)} copy-done((bf16[2,128,64]{2,1,0:T(8,128)(2,1)S(1)}, bf16[2,128,64]{2,1,0:T(8,128)(2,1)}, u32[]{:S(2)}) %copy-start.7) | copy-done | bytes 32792
  7.9 0.0 copy-start.8
  7.9 0.8 %copy-done.8 = bf16[2,64,128]{2,1,0:T(8,128)(2,1)S(1)} copy-done((bf16[2,64,128]{2,1,0:T(8,128)(2,1)S(1)}, bf16[2,64,128]{2,1,0:T(8,128)(2,1)}, u32[]{:S(2)}) %copy-start.8) | copy-done | bytes 32792
  8.7 0.0 copy-start.9
  8.7 0.8 %copy-done.9 = bf16[2,64,128]{2,1,0:T(8,128)(2,1)S(1)} copy-done((bf16[2,64,128]{2,1,0:T(8,128)(2,1)S(1)}, bf16[2,64,128]{2,1,0:T(8,128)(2,1)}, u32[]{:S(2)}) %copy-start.9) | copy-done | bytes 32792
  9.4 62.0 %iteration.1 = f32[1,2,2,4,128,128]{5,4,3,2,1,0:T(8,128)S(1)} custom-call(f32[1,2,2,4,128,128]{5,4,3,2,1,0:T(8,128)S(1)} %copy-done, f32[2,4,128,128]{3,2,1,0:T(8,128)S(1)} %copy-done.1, bf16[2,128,256]{2,1,0:T(8,128)(2,1)S(1)} %copy-done.6, bf16[2,256,128]{2,1,0:T(8,128)(2,1)S(1)} %copy-done.5, bf16[2,64,128]{2,1,0:T(8,128)(2,1)S(1)} %copy-done.9, ...), custom_call_target="tpu_custom_call" | custom-call | tf_op jit(solution)/shard_map/iteration/pallas_call | solution.py:515
  71.4 1.0 %copy.12 = f32[1,2,2,4,128,128]{5,4,3,2,1,0:T(8,128)} copy(f32[1,2,2,4,128,128]{5,4,3,2,1,0:T(8,128)S(1)} %iteration.1) | data formatting | bytes 2097152
Async XLA Ops:
  0.0 1.2 %copy-start = (f32[1,2,2,4,128,128]{5,4,3,2,1,0:T(8,128)S(1)}, f32[1,2,2,4,128,128]{5,4,3,2,1,0:T(8,128)}, u32[]{:S(2)}) copy-start(f32[1,2,2,4,128,128]{5,4,3,2,1,0:T(8,128)} %nodes.1) | copy-start | bytes 3145732
  1.2 1.0 %copy-start.1 = (f32[2,4,128,128]{3,2,1,0:T(8,128)S(1)}, f32[2,4,128,128]{3,2,1,0:T(8,128)}, u32[]{:S(2)}) copy-start(f32[2,4,128,128]{3,2,1,0:T(8,128)} %initial.1) | copy-start | bytes 1572868
  2.3 1.0 %copy-start.2 = (f32[2,8,64,128]{3,2,1,0:T(8,128)S(1)}, f32[2,8,64,128]{3,2,1,0:T(8,128)}, u32[]{:S(2)}) copy-start(f32[2,8,64,128]{3,2,1,0:T(8,128)} %constant.23.clone.p_h) | copy-start | bytes 1572868
  3.3 1.0 %copy-start.3 = (bf16[2,512,256]{2,1,0:T(8,128)(2,1)S(1)}, bf16[2,512,256]{2,1,0:T(8,128)(2,1)}, u32[]{:S(2)}) copy-start(bf16[2,512,256]{2,1,0:T(8,128)(2,1)} %constant.22.clone.vx_h) | copy-start | bytes 1572868
  4.4 0.9 %copy-start.4 = (bf16[2,128,256]{2,1,0:T(8,128)(2,1)S(1)}, bf16[2,128,256]{2,1,0:T(8,128)(2,1)}, u32[]{:S(2)}) copy-start(bf16[2,128,256]{2,1,0:T(8,128)(2,1)} %constant.21.clone.vy_h) | copy-start | bytes 393220
  5.3 0.9 %copy-start.5 = (bf16[2,256,128]{2,1,0:T(8,128)(2,1)S(1)}, bf16[2,256,128]{2,1,0:T(8,128)(2,1)}, u32[]{:S(2)}) copy-start(bf16[2,256,128]{2,1,0:T(8,128)(2,1)} %constant.17.clone.fy_h) | copy-start | bytes 393220
  6.2 0.9 %copy-start.6 = (bf16[2,128,256]{2,1,0:T(8,128)(2,1)S(1)}, bf16[2,128,256]{2,1,0:T(8,128)(2,1)}, u32[]{:S(2)}) copy-start(bf16[2,128,256]{2,1,0:T(8,128)(2,1)} %constant.16.clone.fx_h) | copy-start | bytes 393220
  7.1 0.8 %copy-start.7 = (bf16[2,128,64]{2,1,0:T(8,128)(2,1)S(1)}, bf16[2,128,64]{2,1,0:T(8,128)(2,1)}, u32[]{:S(2)}) copy-start(bf16[2,128,64]{2,1,0:T(8,128)(2,1)} %constant.20.clone.nz_h) | copy-start | bytes 98308
  7.9 0.8 %copy-start.8 = (bf16[2,64,128]{2,1,0:T(8,128)(2,1)S(1)}, bf16[2,64,128]{2,1,0:T(8,128)(2,1)}, u32[]{:S(2)}) copy-start(bf16[2,64,128]{2,1,0:T(8,128)(2,1)} %constant.19.clone.m1_h) | copy-start | bytes 98308
  8.7 0.8 %copy-start.9 = (bf16[2,64,128]{2,1,0:T(8,128)(2,1)S(1)}, bf16[2,64,128]{2,1,0:T(8,128)(2,1)}, u32[]{:S(2)}) copy-start(bf16[2,64,128]{2,1,0:T(8,128)(2,1)} %constant.18.clone.m0_h) | copy-start | bytes 98308

commit v2 on v1

--- a/solution.py
+++ b/solution.py
@@ -105,8 +105,8 @@
     nodes, initial, fx_h, fy_h, m0_h, m1_h, nz_h, vy_h, vx_h, p_h,
     out,
     u, s1, s2, a, g, fx, fy, m0, m1, nz, vy, vx, pw,
-    spec, c2in, gather, e2, xin, tot, zin, back, pre, fine, fin,
-    ssem, lsem, r_u0, r_h, r_u0h, r_s1, r_c2, r_in, r_x, r_z, r_b, r_f,
+    spec, c2out, c2in, gather, e2, xin, tot, zin, back, pre, fine, fin,
+    ssem, lsem, r_u0, r_h, r_u0h, r_s1, r_c2, r_in, r_x, r_z, r_b, r_f, credit,
 ):
     count, spaces, chips_x, chips_z, n = shape
     tm, sp = lax.axis_index("tm"), lax.axis_index("space")
@@ -136,13 +136,15 @@
     has_next, has_prior = tm < count - 1, tm > 0
     nxt = (lax.rem(tm + 1, count), sp)
     prv = (lax.rem(tm + count - 1, count), sp)
-    yc = [(d % spaces, d // spaces) for d in range(1, 2 * spaces)]
+    ring = sorted(range(spaces), key=lambda d: -min(d, spaces - d))
+    yc = [(d, c) for d in ring for c in (1, 0) if (d, c) != (0, 0)]
 
     def owner(d):
         return lax.rem(sp + d[0], spaces), lax.rem(core + d[1], 2)
 
-    x_peers = [lax.rem(cx + d, chips_x) for d in range(1, chips_x)]
-    z_peers = [lax.rem(cz + d, chips_z) for d in range(1, chips_z)]
+    x_peers = [lax.rem(cx + d, chips_x) for d in (2, 1, 3) if d < chips_x]
+    if chips_x == 2:
+        x_peers = [1 - cx]
 
     loads = [
         pltpu.make_async_copy(nodes.at[0, 0], u.at[1, :, pl.ds(1, 4)], lsem.at[0]),
@@ -168,25 +170,64 @@
             ).start()
 
     barrier = pltpu.get_barrier_semaphore()
-    peers = []
-    for d in yc:
-        y, c = owner(d)
-        peers.append((chip * 2 + c, y))
-    peers += [(at(cz, x, core), sp) for x in x_peers]
-    peers += [(at(z, cx, core), sp) for z in z_peers]
-    peers.append((lax.rem(tm + count - 1 + 2 * core, count), sp))
-    for peer in peers:
-        pl.semaphore_signal(barrier, 1, device_id=peer, device_id_type=MESH)
-    pl.semaphore_wait(barrier, len(peers))
+    sibling = tm + 1 - 2 * core
+    crosses = jnp.where(core == 1, cx == chips_x - 1, cx == 0)
+    beside = lax.rem(tm + count - 1 + 2 * core, count)
+    has_beside = jnp.where(core == 1, has_next, has_prior)
+
+    def greet(t, y):
+        pl.semaphore_signal(barrier, 1, device_id=(t, y), device_id_type=MESH)
+
+    def answer(which, t, y):
+        pl.semaphore_signal(credit.at[which], 1, device_id=(t, y), device_id_type=MESH)
+
+    def waits_for(which, answers):
+        pl.when(answers > 0)(lambda: pl.semaphore_wait(credit.at[which], answers))
+
+    def over(lower, upper, work):
+        def step(i, carry):
+            work(i)
+            return carry
+
+        lax.fori_loop(lower, upper, step, 0)
+
+    def far_columns(y, call):
+        call(sibling, y)
+        pl.when((y != sp + 1) & (y != sp - 1))(lambda: call(tm, y))
+
+    pl.when(has_hi)(lambda: greet(tm, hi[1]))
+    pl.when(has_lo)(lambda: greet(tm, lo[1]))
+    greet(sibling, sp)
+    pl.when(has_beside & (~crosses | (core == 1)))(lambda: greet(beside, sp))
+    over(sp + 1, spaces, lambda y: far_columns(y, greet))
+    over(cx + 1, chips_x, lambda x: greet(at(cz, x, core), sp))
+    over(cz + 1, chips_z, lambda z: greet(at(z, cx, core), sp))
+
+    def one(flag):
+        return jnp.where(flag, 1, 0)
+
+    below_far = 2 * sp - one(has_lo)
+    above_far = 2 * (spaces - 1 - sp) - one(has_hi)
+    pl.semaphore_wait(
+        barrier,
+        one(has_lo) + one(has_hi) + 1 + one(has_beside & (~crosses | (core == 0)))
+        + below_far + cx + cz,
+    )
+    pl.when(has_beside & crosses & (core == 0))(lambda: answer(3, beside, sp))
 
     for node in (2, 1):
         send(nodes.at[0, node - 1, :, 3], u.at[node, :, 0], r_h.at[node - 1, 0], hi, has_hi)
         send(nodes.at[0, node - 1, :, 0], u.at[node, :, 5], r_h.at[node - 1, 1], lo, has_lo)
+    waits_for(3, one(has_beside & crosses & (core == 1)))
     for i, (z, length) in enumerate(pieces):
         send(
             nodes.at[0, 1, :, pl.ds(z, length)], u.at[0, :, pl.ds(1 + z, length)],
             r_u0.at[i], nxt, has_next,
         )
+
+    over(0, sp, lambda y: far_columns(y, functools.partial(answer, 0)))
+    over(0, cx, lambda x: answer(1, at(cz, x, core), sp))
+    over(0, cz, lambda z: answer(2, at(z, cx, core), sp))
 
     zero = jnp.zeros((n, n), jnp.float32)
     for s in range(2):
@@ -360,36 +401,47 @@
         for s in range(2):
             at_s = slice(s * n, (s + 1) * n)
             wide = jnp.concatenate([along_x[: n // 2, at_s], along_x[n // 2 :, at_s]], axis=1)
-            spec[s, i] = right(wide, fy)
+            modes = right(wide, fy)
+            if i == 3:
+                c2out[s] = modes
+            else:
+                spec[s, :, (i + 2) % 3] = modes.reshape(spaces, part, n)
 
     part = n // 2 // spaces
     to_modes(3)
-    send(spec.at[:, 3], c2in, r_c2, nxt, has_next)
-    for i in (1, 2, 0):
-        to_modes(i)
+    send(c2out, c2in, r_c2, nxt, has_next)
+    to_modes(1)
+    to_modes(2)
+    waits_for(0, above_far)
+
+    def exchange(k, fields):
+        for d in yc:
+            y, c = owner(d)
+            send(
+                spec.at[c, y, fields], gather.at[core, sp, fields], r_in.at[k, core, sp],
+                (chip * 2 + c, y),
+            )
+
+    exchange(0, pl.ds(0, 2))
+    to_modes(0)
     pl.when(has_prior)(lambda: arrived(c2in, r_c2))
     for s in range(2):
-        spec[s, 0] = spec[s, 0] + c2in[s]
-
-    def mine(y):
-        return pl.ds(pl.multiple_of(y * part, part), part)
-
-    for d in yc:
-        y, c = owner(d)
-        send(spec.at[c, pl.ds(0, 3), mine(y)], gather.at[core, :, sp], r_in.at[core, sp], (chip * 2 + c, y))
-    gather[core, :, sp] = spec[core, 0:3, mine(sp)]
-    for d in yc:
-        y, c = owner(d)
-        arrived(gather.at[c, :, y], r_in.at[c, y])
+        spec[s, :, 2] = spec[s, :, 2] + c2in[s].reshape(spaces, part, n)
+    exchange(1, pl.ds(2, 1))
+    gather[core, sp] = spec[core, sp]
+    for k, fields in ((0, pl.ds(0, 2)), (1, pl.ds(2, 1))):
+        for d in yc:
+            y, c = owner(d)
+            arrived(gather.at[c, y, fields], r_in.at[k, c, y])
 
     m = n // 2
     power = pw[...]
     square = power * power
     d0, d1 = [], []
     for c in range(2):
-        own = [gather[c, i].reshape(m, n) for i in range(3)]
-        d0.append(left(m0, jnp.concatenate([own[0], own[2]], axis=0)))
-        d1.append(left(m1, jnp.concatenate([own[1], own[2]], axis=0)))
+        own = [gather[c, :, i].reshape(m, n) for i in range(3)]
+        d0.append(left(m0, jnp.concatenate([own[2], own[1]], axis=0)))
+        d1.append(left(m1, jnp.concatenate([own[0], own[1]], axis=0)))
     e = [power * (power * d0[c] + d1[c]) for c in range(2)]
     e2[...] = square * e[0] + e[1]
 
@@ -398,6 +450,7 @@
     def shared(x):
         return pl.ds(pl.multiple_of(x * share, share), share)
 
+    waits_for(1, chips_x - 1 - cx)
     for x in x_peers:
         send(e2.at[shared(x)], xin.at[cx], r_x.at[cx], (at(cz, x, core), sp))
     xin[cx] = e2[shared(cx)]
@@ -415,14 +468,15 @@
         running = p4 * running + xin[x]
         power_x = power_x * p4
     tot[...] = running
-    for z in z_peers:
-        send(tot, zin.at[cz], r_z.at[cz], (at(z, cx, core), sp))
-    zin[cz] = running
-    for z in z_peers:
+    waits_for(2, chips_z - 1 - cz)
+    for z in reversed(range(1, chips_z)):
+        send(tot, zin.at[cz], r_z.at[cz], (at(z, cx, core), sp), z > cz)
+
+    def add_group(z, earlier):
         arrived(zin.at[z], r_z.at[z])
-    earlier = jnp.zeros((share, n), jnp.float32)
-    for z in range(chips_z):
-        earlier = jnp.where(z < cz, power_x * earlier + zin[z], earlier)
+        return power_x * earlier + zin[z]
+
+    earlier = lax.fori_loop(0, cz, add_group, jnp.zeros((share, n), jnp.float32))
     for x in range(chips_x):
         back[x] = ahead[x] * earlier + before[x]
     for x in x_peers:
@@ -435,24 +489,20 @@
     for c in range(2):
         for f, source in enumerate((d0[c], d1[c])):
             change = power * (change + source)
-            fine[c, f] = left(nz, change)
-    rows_back = 2 * part
-
-    def planes(y):
-        return pl.ds(pl.multiple_of(y * rows_back, rows_back), rows_back)
+            fine[c, :, f] = left(nz, change).reshape(spaces, 2 * part, n)
 
     for d in yc:
         y, c = owner(d)
-        send(fine.at[c, :, planes(y)], fin.at[:, core, sp], r_f.at[core, sp], (chip * 2 + c, y))
-    fin[:, core, sp] = fine[core, :, planes(sp)]
+        send(fine.at[c, y], fin.at[core, sp], r_f.at[core, sp], (chip * 2 + c, y))
+    fin[core, sp] = fine[core, sp]
     for d in yc:
         y, c = owner(d)
-        arrived(fin.at[:, c, y], r_f.at[c, y])
+        arrived(fin.at[c, y], r_f.at[c, y])
 
     for f in range(2):
         tall = []
         for s in range(2):
-            wide = right(fin[f, s].reshape(n, n), vy)
+            wide = right(fin[s, :, f].reshape(n, n), vy)
             tall.append(jnp.concatenate([wide[:, :n], wide[:, n:]], axis=0))
         refined = left(vx, jnp.concatenate(tall, axis=1))
         for s in range(2):
@@ -476,7 +526,7 @@
     share = m // chips_x
     f32 = jnp.float32
     vmem, sem = pltpu.VMEM, pltpu.SemaphoreType.DMA
-    n_sends = 4 + 3 + 4 + 2 + 1 + 2 * (2 * spaces - 1) + 2 * (chips_x - 1) + chips_z - 1
+    n_sends = 4 + 3 + 4 + 2 + 1 + 3 * (2 * spaces - 1) + 2 * (chips_x - 1) + chips_z - 1
     scratch = [
         vmem((3, 2, 6, n, n), f32),
         vmem((2, 6, n, n), f32),
@@ -487,17 +537,18 @@
     scratch += [vmem(c.shape, jnp.bfloat16) for c in consts[:-1]]
     scratch += [
         vmem((m, n), f32),
-        vmem((2, 4, m, n), f32),
+        vmem((2, spaces, 3, part, n), f32),
         vmem((2, m, n), f32),
-        vmem((2, 3, spaces, part, n), f32),
+        vmem((2, m, n), f32),
+        vmem((2, spaces, 3, part, n), f32),
         vmem((m, n), f32),
         vmem((chips_x, share, n), f32),
         vmem((share, n), f32),
         vmem((chips_z, share, n), f32),
         vmem((chips_x, share, n), f32),
         vmem((m, n), f32),
-        vmem((2, 2, n, n), f32),
-        vmem((2, 2, spaces, 2 * part, n), f32),
+        vmem((2, spaces, 2, 2 * part, n), f32),
+        vmem((2, spaces, 2, 2 * part, n), f32),
         sem((n_sends,)),
         sem((10,)),
         sem((3,)),
@@ -505,12 +556,14 @@
         sem((2,)),
         sem((2,)),
         sem(()),
-        sem((2, spaces)),
+        sem((2, 2, spaces)),
         sem((chips_x,)),
         sem((chips_z,)),
         sem((chips_x,)),
         sem((2, spaces)),
+        pltpu.SemaphoreType.REGULAR((4,)),
     ]
+    operands = [nodes, initial, *[jnp.asarray(c) for c in consts]]
     anywhere = pl.BlockSpec(memory_space=pl.ANY)
     return pl.pallas_call(
         functools.partial(kernel, shape),
@@ -519,10 +572,10 @@
         out_specs=pl.BlockSpec(memory_space=pltpu.VMEM),
         scratch_shapes=scratch,
         compiler_params=pltpu.CompilerParams(
-            collective_id=0, has_side_effects=True, vmem_limit_bytes=48 << 20
+            collective_id=0, has_side_effects=True, vmem_limit_bytes=40 << 20
         ),
         name="iteration",
-    )(nodes, initial, *[jnp.asarray(c) for c in consts])
+    )(*[pltpu.with_memory_space_constraint(x, pltpu.HBM) for x in operands])
 
 
 def solution(mesh):

time: 72.9 us -> 51.7 us (0.71)
  the two profiles are of different devices: /device:TPU:1 before, /device:TPU:384 now
where the time goes in v2:
time: 51.7 us; the launch traced here: 51.3 us
  Pallas kernels  50.4 us (97%)
  local copies, waits for them, and re-layouts  0.97 us (2%)
    pallas_call x1, Pallas kernels, local(): pl.pallas_call(functools.partial(kernel, shape), out_shape=jax.ShapeDtype...  50.4 us

profile of v2, /device:TPU:384, one launch (start us, length us, event | category | flops | bytes accessed | tf_op | source)
XLA Modules:
  0.0 51.3 jit_solution(1773240041525851134)
XLA Ops:
  0.0 50.4 %iteration.1 = f32[1,2,2,4,128,128]{5,4,3,2,1,0:T(8,128)S(1)} custom-call(f32[1,2,2,4,128,128]{5,4,3,2,1,0:T(8,128)} %nodes.1, f32[2,4,128,128]{3,2,1,0:T(8,128)} %initial.1, bf16[2,128,256]{2,1,0:T(8,128)(2,1)} %constant.16.clone.fx_h, bf16[2,256,128]{2,1,0:T(8,128)(2,1)} %constant.17.clone.fy_h, bf16[2,64,128]{2,1,0:T(8,128)(2,1)} %constant.18.clone.m0_h, ...), custom_call_target="tpu_custom_call" | custom-call | tf_op jit(solution)/shard_map/iteration/pallas_call | solution.py:568
  50.4 1.0 %copy.12 = f32[1,2,2,4,128,128]{5,4,3,2,1,0:T(8,128)} copy(f32[1,2,2,4,128,128]{5,4,3,2,1,0:T(8,128)S(1)} %iteration.1) | data formatting | bytes 2097152

commit v3 on v2

--- a/solution.py
+++ b/solution.py
@@ -105,8 +105,8 @@
     nodes, initial, fx_h, fy_h, m0_h, m1_h, nz_h, vy_h, vx_h, p_h,
     out,
     u, s1, s2, a, g, fx, fy, m0, m1, nz, vy, vx, pw,
-    spec, c2out, c2in, gather, e2, xin, tot, zin, back, pre, fine, fin,
-    ssem, lsem, r_u0, r_h, r_u0h, r_s1, r_c2, r_in, r_x, r_z, r_b, r_f, credit,
+    sx, rim, spec, c2out, c2in, gather, e2, xin, tot, zin, fine, fin,
+    ssem, lsem, r_u0, r_h, r_u0h, r_s1, r_c2, r_in, r_x, r_z, r_f, credit,
 ):
     count, spaces, chips_x, chips_z, n = shape
     tm, sp = lax.axis_index("tm"), lax.axis_index("space")
@@ -170,10 +170,21 @@
             ).start()
 
     barrier = pltpu.get_barrier_semaphore()
+
+    def one(flag):
+        return jnp.where(flag, 1, 0)
+
     sibling = tm + 1 - 2 * core
     crosses = jnp.where(core == 1, cx == chips_x - 1, cx == 0)
     beside = lax.rem(tm + count - 1 + 2 * core, count)
     has_beside = jnp.where(core == 1, has_next, has_prior)
+
+    half = chips_z // 2
+    half_at = (cz // half) * half
+    ends = cz == half_at + half - 1
+    z_first = cz + 1
+    z_last = jnp.where(ends, jnp.minimum(half_at + 2 * half, chips_z), half_at + half)
+    z_below = cz - half_at + one(half_at > 0)
 
     def greet(t, y):
         pl.semaphore_signal(barrier, 1, device_id=(t, y), device_id_type=MESH)
@@ -201,17 +212,14 @@
     pl.when(has_beside & (~crosses | (core == 1)))(lambda: greet(beside, sp))
     over(sp + 1, spaces, lambda y: far_columns(y, greet))
     over(cx + 1, chips_x, lambda x: greet(at(cz, x, core), sp))
-    over(cz + 1, chips_z, lambda z: greet(at(z, cx, core), sp))
-
-    def one(flag):
-        return jnp.where(flag, 1, 0)
+    over(z_first, z_last, lambda z: greet(at(z, cx, core), sp))
 
     below_far = 2 * sp - one(has_lo)
     above_far = 2 * (spaces - 1 - sp) - one(has_hi)
     pl.semaphore_wait(
         barrier,
         one(has_lo) + one(has_hi) + 1 + one(has_beside & (~crosses | (core == 0)))
-        + below_far + cx + cz,
+        + below_far + cx + z_below,
     )
     pl.when(has_beside & crosses & (core == 0))(lambda: answer(3, beside, sp))
 
@@ -227,7 +235,8 @@
 
     over(0, sp, lambda y: far_columns(y, functools.partial(answer, 0)))
     over(0, cx, lambda x: answer(1, at(cz, x, core), sp))
-    over(0, cz, lambda z: answer(2, at(z, cx, core), sp))
+    over(half_at, cz, lambda z: answer(2, at(z, cx, core), sp))
+    pl.when(half_at > 0)(lambda: answer(2, at(half_at - 1, cx, core), sp))
 
     zero = jnp.zeros((n, n), jnp.float32)
     for s in range(2):
@@ -315,26 +324,45 @@
     arrived(u.at[0, :, pl.ds(2, 2)], r_u0.at[2])
     for z in (1, 2, 3, 4):
         sum_one(z)
+    edges = ((0, 1, 2, 0), (1, 4, 3, 5))
+    for k, z, inner, _ in edges:
+        for r in chunks:
+            for s in range(2):
+                around, mid = sides(s, z, r)
+                lap = around + a[s, inner, 8 + r : 8 + r + ROWS, :] - 6.0 * mid
+                sx[k, s, r : r + ROWS, :] = rows(s1, s, z, r=r) + DIFFUSE[s] * lap
+                rim[k, s, r : r + ROWS, :] = DIFFUSE[s] * mid
+        if k == 0:
+            send(sx.at[0], s1.at[:, 5], r_s1.at[1], lo, has_lo)
+        else:
+            send(sx.at[1], s1.at[:, 0], r_s1.at[0], hi, has_hi)
     for z in (2, 3):
         diffuse(s1, z, 0)
-    pl.when(has_lo)(lambda: arrived(u.at[1, :, 0], r_h.at[0, 0]))
-    pl.when(has_lo)(lambda: arrived(u.at[0, :, 0], r_u0h.at[0]))
-    sum_one(0, False)
-    diffuse(s1, 1, 0)
-    send(s1.at[:, 1], s1.at[:, 5], r_s1.at[1], lo, has_lo)
-    pl.when(has_hi)(lambda: arrived(u.at[1, :, 5], r_h.at[0, 1]))
-    pl.when(has_hi)(lambda: arrived(u.at[0, :, 5], r_u0h.at[1]))
-    sum_one(5, False)
-    diffuse(s1, 4, 0)
-    send(s1.at[:, 4], s1.at[:, 0], r_s1.at[0], hi, has_hi)
+    for k, z, _, outer in edges:
+        has = (has_lo, has_hi)[k]
+        ready = [(u.at[1, :, outer], r_h.at[0, k]), (u.at[0, :, outer], r_u0h.at[k])]
+        for dst, landed in ready:
+            pl.when(has)(functools.partial(arrived, dst, landed))
+        sum_one(outer, False)
+        for r in chunks:
+            for s in range(2):
+                beyond = a[s, outer, 8 + r : 8 + r + ROWS, :]
+                s1[s, z, r : r + ROWS, :] = sx[k, s, r : r + ROWS, :] + DIFFUSE[s] * beyond
 
     for z in (1, 2, 3, 4):
         sum_two(z)
     for z in (2, 3):
         diffuse(s2, z, 1)
-    pl.when(has_lo)(lambda: arrived(s1.at[:, 0], r_s1.at[0]))
-    pl.when(has_hi)(lambda: arrived(s1.at[:, 5], r_s1.at[1]))
+
+    def complete(k, outer):
+        arrived(s1.at[:, outer], r_s1.at[k])
+        for r in chunks:
+            for s in range(2):
+                s1[s, outer, r : r + ROWS, :] = rows(s1, s, outer, r=r) + rim[k, s, r : r + ROWS, :]
+
+    pl.when(has_lo)(lambda: complete(0, 0))
     sum_two(0, False)
+    pl.when(has_hi)(lambda: complete(1, 5))
     sum_two(5, False)
     diffuse(s2, 1, 1)
     diffuse(s2, 4, 1)
@@ -445,47 +473,55 @@
     e = [power * (power * d0[c] + d1[c]) for c in range(2)]
     e2[...] = square * e[0] + e[1]
 
-    share = m // chips_x
-
-    def shared(x):
-        return pl.ds(pl.multiple_of(x * share, share), share)
-
     waits_for(1, chips_x - 1 - cx)
     for x in x_peers:
-        send(e2.at[shared(x)], xin.at[cx], r_x.at[cx], (at(cz, x, core), sp))
-    xin[cx] = e2[shared(cx)]
+        send(e2, xin.at[cx], r_x.at[cx], (at(cz, x, core), sp))
+    xin[cx] = e2[...]
+    p4 = square * square
+    p16 = p4
+    for _ in range(chips_x - 1):
+        p16 = p16 * p4
     for x in x_peers:
         arrived(xin.at[x], r_x.at[x])
-    p1 = pw[shared(cx)]
-    p2 = p1 * p1
-    p4 = p2 * p2
-    running = jnp.zeros((share, n), jnp.float32)
-    before, ahead = [], []
-    power_x = jnp.ones((share, n), jnp.float32)
-    for x in range(chips_x):
-        before.append(running)
-        ahead.append(power_x)
-        running = p4 * running + xin[x]
-        power_x = power_x * p4
-    tot[...] = running
-    waits_for(2, chips_z - 1 - cz)
-    for z in reversed(range(1, chips_z)):
-        send(tot, zin.at[cz], r_z.at[cz], (at(z, cx, core), sp), z > cz)
+
+    def add_chip(x, carry):
+        running, ahead = carry
+        return p4 * running + xin[x], p4 * ahead
+
+    start = (jnp.zeros((m, n), jnp.float32), jnp.ones((m, n), jnp.float32))
+    before, ahead = lax.fori_loop(0, cx, add_chip, start)
+    total, _ = lax.fori_loop(cx, chips_x, add_chip, (before, ahead))
+    waits_for(2, z_last - z_first)
+
+    later = [(cz + d, at(jnp.minimum(cz + d, chips_z - 1), cx, core)) for d in range(1, half + 1)]
+
+    @pl.when(~ends)
+    def _():
+        tot[...] = total
+
+    for z, t in later[:-1]:
+        send(tot, zin.at[cz - half_at], r_z.at[cz - half_at], (t, sp), ~ends & (z < z_last))
+
+    @pl.when(half_at == 0)
+    def _():
+        zin[half] = jnp.zeros((m, n), jnp.float32)
+
+    pl.when(half_at > 0)(lambda: arrived(zin.at[half], r_z.at[half]))
 
     def add_group(z, earlier):
         arrived(zin.at[z], r_z.at[z])
-        return power_x * earlier + zin[z]
-
-    earlier = lax.fori_loop(0, cz, add_group, jnp.zeros((share, n), jnp.float32))
-    for x in range(chips_x):
-        back[x] = ahead[x] * earlier + before[x]
-    for x in x_peers:
-        send(back.at[x], pre.at[shared(cx)], r_b.at[cx], (at(cz, x, core), sp))
-    pre[shared(cx)] = back[cx]
-    for x in x_peers:
-        arrived(pre.at[shared(x)], r_b.at[x])
-
-    change = pre[...]
+        return p16 * earlier + zin[z]
+
+    earlier = lax.fori_loop(0, cz - half_at, add_group, zin[half])
+
+    @pl.when(ends)
+    def _():
+        tot[...] = p16 * earlier + total
+
+    for z, t in later:
+        send(tot, zin.at[half], r_z.at[half], (t, sp), ends & (z < z_last))
+
+    change = ahead * earlier + before
     for c in range(2):
         for f, source in enumerate((d0[c], d1[c])):
             change = power * (change + source)
@@ -523,10 +559,9 @@
     consts = tables(n, spaces)
     m = n // 2
     part = m // spaces
-    share = m // chips_x
     f32 = jnp.float32
     vmem, sem = pltpu.VMEM, pltpu.SemaphoreType.DMA
-    n_sends = 4 + 3 + 4 + 2 + 1 + 3 * (2 * spaces - 1) + 2 * (chips_x - 1) + chips_z - 1
+    n_sends = 4 + 3 + 4 + 2 + 1 + 3 * (2 * spaces - 1) + chips_x - 1 + chips_z - 1
     scratch = [
         vmem((3, 2, 6, n, n), f32),
         vmem((2, 6, n, n), f32),
@@ -537,16 +572,16 @@
     scratch += [vmem(c.shape, jnp.bfloat16) for c in consts[:-1]]
     scratch += [
         vmem((m, n), f32),
+        vmem((2, 2, n, n), f32),
+        vmem((2, 2, n, n), f32),
         vmem((2, spaces, 3, part, n), f32),
         vmem((2, m, n), f32),
         vmem((2, m, n), f32),
         vmem((2, spaces, 3, part, n), f32),
         vmem((m, n), f32),
-        vmem((chips_x, share, n), f32),
-        vmem((share, n), f32),
-        vmem((chips_z, share, n), f32),
-        vmem((chips_x, share, n), f32),
+        vmem((chips_x, m, n), f32),
         vmem((m, n), f32),
+        vmem((chips_z // 2 + 1, m, n), f32),
         vmem((2, spaces, 2, 2 * part, n), f32),
         vmem((2, spaces, 2, 2 * part, n), f32),
         sem((n_sends,)),
@@ -558,8 +593,7 @@
         sem(()),
         sem((2, 2, spaces)),
         sem((chips_x,)),
-        sem((chips_z,)),
-        sem((chips_x,)),
+        sem((chips_z // 2 + 1,)),
         sem((2, spaces)),
         pltpu.SemaphoreType.REGULAR((4,)),
     ]

time: 51.7 us -> 48.6 us (0.940)
  the two profiles are of different devices: /device:TPU:384 before, /device:TPU:450 now
where the time goes in v3:
time: 48.6 us; the launch traced here: 48.4 us
  Pallas kernels  47.5 us (98%)
  local copies, waits for them, and re-layouts  0.97 us (2%)
    pallas_call x1, Pallas kernels, local(): pl.pallas_call(functools.partial(kernel, shape), out_shape=jax.ShapeDtype...  47.5 us
    unnamed x1, local copies, waits for them, and re-layouts  0.97 us

profile of v3, /device:TPU:450, one launch (start us, length us, event | category | flops | bytes accessed | tf_op | source)
XLA Modules:
  0.0 48.4 jit_solution(130871069433560445)
XLA Ops:
  0.0 47.5 %iteration.1 = f32[1,2,2,4,128,128]{5,4,3,2,1,0:T(8,128)S(1)} custom-call(f32[1,2,2,4,128,128]{5,4,3,2,1,0:T(8,128)} %nodes.1, f32[2,4,128,128]{3,2,1,0:T(8,128)} %initial.1, bf16[2,128,256]{2,1,0:T(8,128)(2,1)} %constant.16.clone.fx_h, bf16[2,256,128]{2,1,0:T(8,128)(2,1)} %constant.17.clone.fy_h, bf16[2,64,128]{2,1,0:T(8,128)(2,1)} %constant.18.clone.m0_h, ...), custom_call_target="tpu_custom_call" | custom-call | tf_op jit(solution)/shard_map/iteration/pallas_call | solution.py:602
  47.5 1.0 %copy.12 = f32[1,2,2,4,128,128]{5,4,3,2,1,0:T(8,128)} copy(f32[1,2,2,4,128,128]{5,4,3,2,1,0:T(8,128)S(1)} %iteration.1) | data formatting | bytes 2097152

commit v4 on v3

--- a/solution.py
+++ b/solution.py
@@ -58,9 +58,7 @@
             if y < spaces - 1:
                 edge[:, i, y, i, 1] = wz[:, 2 * y + 2]
     own, edge = own.reshape(m, m), edge.reshape(m, m)
-    mats = np.stack(
-        [np.concatenate([own, edge * (DT * S[i][2])], axis=1) for i in range(2)]
-    )
+    mats = np.concatenate([own, edge], axis=1)
     nz = np.kron(sine_table(2 * mz, mz, 2.0), np.eye(per))
     vxy = sine_table(n, m, 2.0)
     vy = np.kron(np.eye(2), vxy.T)
@@ -77,7 +75,7 @@
     lin = np.stack([d * e - k for d, k in zip(DIFFUSE, DECAY)])
     factor = 1.0 / (1.0 - H * lin)
     factor = factor.reshape(2, spaces, m, n).astype(np.float32)
-    return tuple(map(two_parts, (fx, fy, mats[0], mats[1], nz, vy, vx))) + (factor,)
+    return tuple(map(two_parts, (fx, fy, mats, nz, vy, vx))) + (factor,)
 
 
 def split(x):
@@ -102,9 +100,9 @@
 
 def kernel(
     shape,
-    nodes, initial, fx_h, fy_h, m0_h, m1_h, nz_h, vy_h, vx_h, p_h,
+    nodes, initial, fx_h, fy_h, mz_h, nz_h, vy_h, vx_h, p_h,
     out,
-    u, s1, s2, a, g, fx, fy, m0, m1, nz, vy, vx, pw,
+    u, s1, s2, a, g, fx, fy, mz, nz, vy, vx, pw,
     sx, rim, spec, c2out, c2in, gather, e2, xin, tot, zin, fine, fin,
     ssem, lsem, r_u0, r_h, r_u0h, r_s1, r_c2, r_in, r_x, r_z, r_f, credit,
 ):
@@ -128,6 +126,13 @@
         else:
             pl.when(when)(copy.start)
 
+    def finish(first, last=None):
+        for copy, when in sends[first:last]:
+            if when is None:
+                copy.wait_send()
+            else:
+                pl.when(when)(copy.wait_send)
+
     def arrived(dst, sem):
         pltpu.make_async_copy(dst, dst, sem).wait()
 
@@ -151,12 +156,11 @@
         pltpu.make_async_copy(nodes.at[0, 1], u.at[2, :, pl.ds(1, 4)], lsem.at[1]),
         pltpu.make_async_copy(fx_h, fx, lsem.at[2]),
         pltpu.make_async_copy(fy_h, fy, lsem.at[3]),
-        pltpu.make_async_copy(m0_h, m0, lsem.at[4]),
-        pltpu.make_async_copy(m1_h, m1, lsem.at[5]),
-        pltpu.make_async_copy(nz_h, nz, lsem.at[6]),
-        pltpu.make_async_copy(vy_h, vy, lsem.at[7]),
-        pltpu.make_async_copy(vx_h, vx, lsem.at[8]),
-        pltpu.make_async_copy(p_h.at[core, sp], pw, lsem.at[9]),
+        pltpu.make_async_copy(mz_h, mz, lsem.at[4]),
+        pltpu.make_async_copy(nz_h, nz, lsem.at[5]),
+        pltpu.make_async_copy(vy_h, vy, lsem.at[6]),
+        pltpu.make_async_copy(vx_h, vx, lsem.at[7]),
+        pltpu.make_async_copy(p_h.at[core, sp], pw, lsem.at[8]),
     ]
     for load in loads:
         load.start()
@@ -175,7 +179,6 @@
         return jnp.where(flag, 1, 0)
 
     sibling = tm + 1 - 2 * core
-    crosses = jnp.where(core == 1, cx == chips_x - 1, cx == 0)
     beside = lax.rem(tm + count - 1 + 2 * core, count)
     has_beside = jnp.where(core == 1, has_next, has_prior)
 
@@ -209,7 +212,7 @@
     pl.when(has_hi)(lambda: greet(tm, hi[1]))
     pl.when(has_lo)(lambda: greet(tm, lo[1]))
     greet(sibling, sp)
-    pl.when(has_beside & (~crosses | (core == 1)))(lambda: greet(beside, sp))
+    pl.when(has_beside)(lambda: greet(beside, sp))
     over(sp + 1, spaces, lambda y: far_columns(y, greet))
     over(cx + 1, chips_x, lambda x: greet(at(cz, x, core), sp))
     over(z_first, z_last, lambda z: greet(at(z, cx, core), sp))
@@ -218,15 +221,13 @@
     above_far = 2 * (spaces - 1 - sp) - one(has_hi)
     pl.semaphore_wait(
         barrier,
-        one(has_lo) + one(has_hi) + 1 + one(has_beside & (~crosses | (core == 0)))
+        one(has_lo) + one(has_hi) + 1 + one(has_beside)
         + below_far + cx + z_below,
     )
-    pl.when(has_beside & crosses & (core == 0))(lambda: answer(3, beside, sp))
 
     for node in (2, 1):
         send(nodes.at[0, node - 1, :, 3], u.at[node, :, 0], r_h.at[node - 1, 0], hi, has_hi)
         send(nodes.at[0, node - 1, :, 0], u.at[node, :, 5], r_h.at[node - 1, 1], lo, has_lo)
-    waits_for(3, one(has_beside & crosses & (core == 1)))
     for i, (z, length) in enumerate(pieces):
         send(
             nodes.at[0, 1, :, pl.ds(z, length)], u.at[0, :, pl.ds(1 + z, length)],
@@ -312,15 +313,14 @@
 
     loads[0].wait()
     loads[1].wait()
-    even = core == 0
     arrived(u.at[0, :, pl.ds(1, 1)], r_u0.at[0])
     arrived(u.at[0, :, pl.ds(4, 1)], r_u0.at[1])
-    send(u.at[0, :, 4], u.at[0, :, 0], r_u0h.at[0], hi, has_hi & even)
-    send(u.at[0, :, 1], u.at[0, :, 5], r_u0h.at[1], lo, has_lo & even)
+    send(u.at[0, :, 4], u.at[0, :, 0], r_u0h.at[0], hi, has_hi & ~has_prior)
+    send(u.at[0, :, 1], u.at[0, :, 5], r_u0h.at[1], lo, has_lo & ~has_prior)
     pl.when(has_lo)(lambda: arrived(u.at[2, :, 0], r_h.at[1, 0]))
     pl.when(has_hi)(lambda: arrived(u.at[2, :, 5], r_h.at[1, 1]))
-    send(u.at[2, :, 0], u.at[0, :, 0], r_u0h.at[0], nxt, has_lo & even)
-    send(u.at[2, :, 5], u.at[0, :, 5], r_u0h.at[1], nxt, has_hi & even)
+    send(u.at[2, :, 0], u.at[0, :, 0], r_u0h.at[0], nxt, has_lo & has_next)
+    send(u.at[2, :, 5], u.at[0, :, 5], r_u0h.at[1], nxt, has_hi & has_next)
     arrived(u.at[0, :, pl.ds(2, 2)], r_u0.at[2])
     for z in (1, 2, 3, 4):
         sum_one(z)
@@ -423,23 +423,32 @@
     for load in loads[2:]:
         load.wait()
 
-    def to_modes(i):
-        both = jnp.concatenate([g[i, 0], g[i, 1]], axis=0)
-        along_x = left(fx, both)
+    def to_modes(fields):
+        both = [jnp.concatenate([g[i, 0], g[i, 1]], axis=0) for i in fields]
+        along_x = left(fx, jnp.concatenate(both, axis=1))
+        half_rows = n // 2
+        wide = jnp.concatenate(
+            [
+                jnp.concatenate(
+                    [along_x[:half_rows, k * n : (k + 1) * n], along_x[half_rows:, k * n : (k + 1) * n]],
+                    axis=1,
+                )
+                for k in range(2 * len(fields))
+            ],
+            axis=0,
+        )
+        modes = right(wide, fy)
+        return [modes[k * half_rows : (k + 1) * half_rows] for k in range(2 * len(fields))]
+
+    part = n // 2 // spaces
+    ends_modes = to_modes([3])
+    for s in range(2):
+        c2out[s] = ends_modes[s]
+    send(c2out, c2in, r_c2, nxt, has_next)
+    others = to_modes([1, 2, 0])
+    for i in range(3):
         for s in range(2):
-            at_s = slice(s * n, (s + 1) * n)
-            wide = jnp.concatenate([along_x[: n // 2, at_s], along_x[n // 2 :, at_s]], axis=1)
-            modes = right(wide, fy)
-            if i == 3:
-                c2out[s] = modes
-            else:
-                spec[s, :, (i + 2) % 3] = modes.reshape(spaces, part, n)
-
-    part = n // 2 // spaces
-    to_modes(3)
-    send(c2out, c2in, r_c2, nxt, has_next)
-    to_modes(1)
-    to_modes(2)
+            spec[s, :, i] = others[2 * i + s].reshape(spaces, part, n)
     waits_for(0, above_far)
 
     def exchange(k, fields):
@@ -450,14 +459,12 @@
                 (chip * 2 + c, y),
             )
 
-    exchange(0, pl.ds(0, 2))
-    to_modes(0)
     pl.when(has_prior)(lambda: arrived(c2in, r_c2))
     for s in range(2):
         spec[s, :, 2] = spec[s, :, 2] + c2in[s].reshape(spaces, part, n)
-    exchange(1, pl.ds(2, 1))
+    exchange(0, pl.ds(0, 3))
     gather[core, sp] = spec[core, sp]
-    for k, fields in ((0, pl.ds(0, 2)), (1, pl.ds(2, 1))):
+    for k, fields in ((0, pl.ds(0, 3)),):
         for d in yc:
             y, c = owner(d)
             arrived(gather.at[c, y, fields], r_in.at[k, c, y])
@@ -465,11 +472,14 @@
     m = n // 2
     power = pw[...]
     square = power * power
-    d0, d1 = [], []
+    columns = []
     for c in range(2):
         own = [gather[c, :, i].reshape(m, n) for i in range(3)]
-        d0.append(left(m0, jnp.concatenate([own[2], own[1]], axis=0)))
-        d1.append(left(m1, jnp.concatenate([own[0], own[1]], axis=0)))
+        for i, field in ((0, own[2]), (1, own[0])):
+            columns.append(jnp.concatenate([field, (DT * S[i][2]) * own[1]], axis=0))
+    modes = left(mz, jnp.concatenate(columns, axis=1))
+    d0 = [modes[:, 2 * c * n : (2 * c + 1) * n] for c in range(2)]
+    d1 = [modes[:, (2 * c + 1) * n : (2 * c + 2) * n] for c in range(2)]
     e = [power * (power * d0[c] + d1[c]) for c in range(2)]
     e2[...] = square * e[0] + e[1]
 
@@ -522,24 +532,33 @@
         send(tot, zin.at[half], r_z.at[half], (t, sp), ends & (z < z_last))
 
     change = ahead * earlier + before
+    changes = []
     for c in range(2):
-        for f, source in enumerate((d0[c], d1[c])):
+        for source in (d0[c], d1[c]):
             change = power * (change + source)
-            fine[c, :, f] = left(nz, change).reshape(spaces, 2 * part, n)
-
+            changes.append(change)
+    at_planes = left(nz, jnp.concatenate(changes, axis=1))
+    for c in range(2):
+        for f in range(2):
+            piece = at_planes[:, (2 * c + f) * n : (2 * c + f + 1) * n]
+            fine[c, :, f] = piece.reshape(spaces, 2 * part, n)
+    started = len(sends)
     for d in yc:
         y, c = owner(d)
         send(fine.at[c, y], fin.at[core, sp], r_f.at[core, sp], (chip * 2 + c, y))
     fin[core, sp] = fine[core, sp]
+    finish(0, started)
     for d in yc:
         y, c = owner(d)
         arrived(fin.at[c, y], r_f.at[c, y])
 
+    received = [fin[s, :, f].reshape(n, n) for f in range(2) for s in range(2)]
+    wide = right(jnp.concatenate(received, axis=0), vy)
     for f in range(2):
         tall = []
         for s in range(2):
-            wide = right(fin[s, :, f].reshape(n, n), vy)
-            tall.append(jnp.concatenate([wide[:, :n], wide[:, n:]], axis=0))
+            rows_of = wide[(2 * f + s) * n : (2 * f + s + 1) * n]
+            tall.append(jnp.concatenate([rows_of[:, :n], rows_of[:, n:]], axis=0))
         refined = left(vx, jnp.concatenate(tall, axis=1))
         for s in range(2):
             for z in range(4):
@@ -547,11 +566,7 @@
                 swept = s1[s, z + 1] if f == 0 else s2[s, z]
                 out[0, f, s, z] = swept + piece
 
-    for copy, when in sends:
-        if when is None:
-            copy.wait_send()
-        else:
-            pl.when(when)(copy.wait_send)
+    finish(started)
 
 
 def local(shape, nodes, initial):
@@ -585,7 +600,7 @@
         vmem((2, spaces, 2, 2 * part, n), f32),
         vmem((2, spaces, 2, 2 * part, n), f32),
         sem((n_sends,)),
-        sem((10,)),
+        sem((9,)),
         sem((3,)),
         sem((2, 2)),
         sem((2,)),
@@ -595,7 +610,7 @@
         sem((chips_x,)),
         sem((chips_z // 2 + 1,)),
         sem((2, spaces)),
-        pltpu.SemaphoreType.REGULAR((4,)),
+        pltpu.SemaphoreType.REGULAR((3,)),
     ]
     operands = [nodes, initial, *[jnp.asarray(c) for c in consts]]
     anywhere = pl.BlockSpec(memory_space=pl.ANY)

time: 48.6 us -> 46.9 us (0.965)
  Pallas kernels: 47.5 us -> 45.7 us
    pallas_call x1, Pallas kernels: 47.5 us -> 45.7 us  [local(): pl.pallas_call(functools.partial(kernel, shape), out_shape=jax.ShapeDtype...]
where the time goes in v4:
time: 46.9 us; the launch traced here: 46.7 us
  Pallas kernels  45.7 us (97%)
  local copies, waits for them, and re-layouts  0.97 us (2%)
    pallas_call x1, Pallas kernels, local(): pl.pallas_call(functools.partial(kernel, shape), out_shape=jax.ShapeDtype...  45.7 us
    unnamed x1, local copies, waits for them, and re-layouts  0.97 us

profile of v4, /device:TPU:450, one launch (start us, length us, event | category | flops | bytes accessed | tf_op | source)
XLA Modules:
  0.0 46.7 jit_solution(1506384450605061013)
XLA Ops:
  0.0 45.7 %iteration.1 = f32[1,2,2,4,128,128]{5,4,3,2,1,0:T(8,128)S(1)} custom-call(f32[1,2,2,4,128,128]{5,4,3,2,1,0:T(8,128)} %nodes.1, f32[2,4,128,128]{3,2,1,0:T(8,128)} %initial.1, bf16[2,128,256]{2,1,0:T(8,128)(2,1)} %constant.14.clone.fx_h, bf16[2,256,128]{2,1,0:T(8,128)(2,1)} %constant.15.clone.fy_h, bf16[2,64,128]{2,1,0:T(8,128)(2,1)} %constant.16.clone.mz_h, ...), custom_call_target="tpu_custom_call" | custom-call | tf_op jit(solution)/shard_map/iteration/pallas_call | solution.py:617
  45.8 1.0 %copy.11 = f32[1,2,2,4,128,128]{5,4,3,2,1,0:T(8,128)} copy(f32[1,2,2,4,128,128]{5,4,3,2,1,0:T(8,128)S(1)} %iteration.1) | data formatting | bytes 2097152

commit v5 on v4

--- a/solution.py
+++ b/solution.py
@@ -164,14 +164,11 @@
     ]
     for load in loads:
         load.start()
-    pieces = [(0, 1), (3, 1), (1, 2)]
+    whole = pl.ds(1, 4)
 
     @pl.when(tm == 0)
     def _():
-        for i, (z, length) in enumerate(pieces):
-            pltpu.make_async_copy(
-                initial.at[:, pl.ds(z, length)], u.at[0, :, pl.ds(1 + z, length)], r_u0.at[i]
-            ).start()
+        pltpu.make_async_copy(initial, u.at[0, :, whole], r_u0).start()
 
     barrier = pltpu.get_barrier_semaphore()
 
@@ -225,15 +222,10 @@
         + below_far + cx + z_below,
     )
 
+    send(nodes.at[0, 1], u.at[0, :, whole], r_u0, nxt, has_next)
     for node in (2, 1):
         send(nodes.at[0, node - 1, :, 3], u.at[node, :, 0], r_h.at[node - 1, 0], hi, has_hi)
         send(nodes.at[0, node - 1, :, 0], u.at[node, :, 5], r_h.at[node - 1, 1], lo, has_lo)
-    for i, (z, length) in enumerate(pieces):
-        send(
-            nodes.at[0, 1, :, pl.ds(z, length)], u.at[0, :, pl.ds(1 + z, length)],
-            r_u0.at[i], nxt, has_next,
-        )
-
     over(0, sp, lambda y: far_columns(y, functools.partial(answer, 0)))
     over(0, cx, lambda x: answer(1, at(cz, x, core), sp))
     over(half_at, cz, lambda z: answer(2, at(z, cx, core), sp))
@@ -313,15 +305,13 @@
 
     loads[0].wait()
     loads[1].wait()
-    arrived(u.at[0, :, pl.ds(1, 1)], r_u0.at[0])
-    arrived(u.at[0, :, pl.ds(4, 1)], r_u0.at[1])
-    send(u.at[0, :, 4], u.at[0, :, 0], r_u0h.at[0], hi, has_hi & ~has_prior)
-    send(u.at[0, :, 1], u.at[0, :, 5], r_u0h.at[1], lo, has_lo & ~has_prior)
     pl.when(has_lo)(lambda: arrived(u.at[2, :, 0], r_h.at[1, 0]))
     pl.when(has_hi)(lambda: arrived(u.at[2, :, 5], r_h.at[1, 1]))
     send(u.at[2, :, 0], u.at[0, :, 0], r_u0h.at[0], nxt, has_lo & has_next)
     send(u.at[2, :, 5], u.at[0, :, 5], r_u0h.at[1], nxt, has_hi & has_next)
-    arrived(u.at[0, :, pl.ds(2, 2)], r_u0.at[2])
+    arrived(u.at[0, :, whole], r_u0)
+    send(u.at[0, :, 4], u.at[0, :, 0], r_u0h.at[0], hi, has_hi & ~has_prior)
+    send(u.at[0, :, 1], u.at[0, :, 5], r_u0h.at[1], lo, has_lo & ~has_prior)
     for z in (1, 2, 3, 4):
         sum_one(z)
     edges = ((0, 1, 2, 0), (1, 4, 3, 5))
@@ -367,6 +357,36 @@
     diffuse(s2, 1, 1)
     diffuse(s2, 4, 1)
 
+    for load in loads[2:]:
+        load.wait()
+
+    def to_modes(fields):
+        both = [jnp.concatenate([g[i, 0], g[i, 1]], axis=0) for i in fields]
+        along_x = left(fx, jnp.concatenate(both, axis=1))
+        half_rows = n // 2
+        wide = jnp.concatenate(
+            [
+                jnp.concatenate(
+                    [along_x[:half_rows, k * n : (k + 1) * n], along_x[half_rows:, k * n : (k + 1) * n]],
+                    axis=1,
+                )
+                for k in range(2 * len(fields))
+            ],
+            axis=0,
+        )
+        modes = right(wide, fy)
+        return [modes[k * half_rows : (k + 1) * half_rows] for k in range(2 * len(fields))]
+
+    part = n // 2 // spaces
+    for j in range(2):
+        for r in chunks:
+            for s in range(2):
+                at_s = slice(s * n, (s + 1) * n)
+                g[3, j, r : r + ROWS, at_s] = rows(s2, s, 2 * j, r=r) + rows(s2, s, 2 * j + 1, r=r)
+    ends_modes = to_modes([3])
+    for s in range(2):
+        c2out[s] = ends_modes[s]
+    send(c2out, c2in, r_c2, nxt, has_next)
     is_first = jnp.where(tm == 0, 1.0, 0.0)
     for i in range(2):
         for j in range(2):
@@ -418,33 +438,7 @@
             for s in range(2):
                 at_s = slice(s * n, (s + 1) * n)
                 g[2, j, r : r + ROWS, at_s] = DIFFUSE[s] * rows(s2, s, 3 * j, r=r)
-                g[3, j, r : r + ROWS, at_s] = rows(s2, s, 2 * j, r=r) + rows(s2, s, 2 * j + 1, r=r)
-
-    for load in loads[2:]:
-        load.wait()
-
-    def to_modes(fields):
-        both = [jnp.concatenate([g[i, 0], g[i, 1]], axis=0) for i in fields]
-        along_x = left(fx, jnp.concatenate(both, axis=1))
-        half_rows = n // 2
-        wide = jnp.concatenate(
-            [
-                jnp.concatenate(
-                    [along_x[:half_rows, k * n : (k + 1) * n], along_x[half_rows:, k * n : (k + 1) * n]],
-                    axis=1,
-                )
-                for k in range(2 * len(fields))
-            ],
-            axis=0,
-        )
-        modes = right(wide, fy)
-        return [modes[k * half_rows : (k + 1) * half_rows] for k in range(2 * len(fields))]
-
-    part = n // 2 // spaces
-    ends_modes = to_modes([3])
-    for s in range(2):
-        c2out[s] = ends_modes[s]
-    send(c2out, c2in, r_c2, nxt, has_next)
+
     others = to_modes([1, 2, 0])
     for i in range(3):
         for s in range(2):
@@ -576,7 +570,7 @@
     part = m // spaces
     f32 = jnp.float32
     vmem, sem = pltpu.VMEM, pltpu.SemaphoreType.DMA
-    n_sends = 4 + 3 + 4 + 2 + 1 + 3 * (2 * spaces - 1) + chips_x - 1 + chips_z - 1
+    n_sends = 4 + 1 + 4 + 2 + 1 + 3 * (2 * spaces - 1) + chips_x - 1 + chips_z - 1
     scratch = [
         vmem((3, 2, 6, n, n), f32),
         vmem((2, 6, n, n), f32),
@@ -601,7 +595,7 @@
         vmem((2, spaces, 2, 2 * part, n), f32),
         sem((n_sends,)),
         sem((9,)),
-        sem((3,)),
+        sem(()),
         sem((2, 2)),
         sem((2,)),
         sem((2,)),

time: 46.9 us -> 46 us (0.981)
  the two profiles are of different devices: /device:TPU:450 before, /device:TPU:384 now
where the time goes in v5:
time: 46 us; the launch traced here: 45.8 us
  Pallas kernels  44.9 us (98%)
  local copies, waits for them, and re-layouts  0.97 us (2%)
    pallas_call x1, Pallas kernels, local(): pl.pallas_call(functools.partial(kernel, shape), out_shape=jax.ShapeDtype...  44.9 us
    unnamed x1, local copies, waits for them, and re-layouts  0.97 us

profile of v5, /device:TPU:384, one launch (start us, length us, event | category | flops | bytes accessed | tf_op | source)
XLA Modules:
  0.0 45.8 jit_solution(16150259630927063895)
XLA Ops:
  0.0 44.9 %iteration.1 = f32[1,2,2,4,128,128]{5,4,3,2,1,0:T(8,128)S(1)} custom-call(f32[1,2,2,4,128,128]{5,4,3,2,1,0:T(8,128)} %nodes.1, f32[2,4,128,128]{3,2,1,0:T(8,128)} %initial.1, bf16[2,128,256]{2,1,0:T(8,128)(2,1)} %constant.14.clone.fx_h, bf16[2,256,128]{2,1,0:T(8,128)(2,1)} %constant.15.clone.fy_h, bf16[2,64,128]{2,1,0:T(8,128)(2,1)} %constant.16.clone.mz_h, ...), custom_call_target="tpu_custom_call" | custom-call | tf_op jit(solution)/shard_map/iteration/pallas_call | solution.py:611
  44.9 1.0 %copy.11 = f32[1,2,2,4,128,128]{5,4,3,2,1,0:T(8,128)} copy(f32[1,2,2,4,128,128]{5,4,3,2,1,0:T(8,128)S(1)} %iteration.1) | data formatting | bytes 2097152

commit v6 on v5

--- a/solution.py
+++ b/solution.py
@@ -279,6 +279,28 @@
                 if base:
                     s1[s, z, r : r + ROWS, :] = pq[0][s] + SIGN[s] * w - DECAY[s] * total
 
+    def begin_one(z):
+        for r in chunks:
+            pq = [[rows(u, i, s, z, r=r) for s in range(2)] for i in (1, 2)]
+            w = sum((DT * S[0][i + 1]) * react(*pq[i]) for i in range(2))
+            for s in range(2):
+                total = sum((DT * S[0][i + 1]) * pq[i][s] for i in range(2))
+                a[s, z, 8 + r : 8 + r + ROWS, :] = total
+                s1[s, z, r : r + ROWS, :] = SIGN[s] * w - DECAY[s] * total
+
+    def end_one(z):
+        weight = DT * S[0][0]
+        for r in chunks:
+            pq = [rows(u, 0, s, z, r=r) for s in range(2)]
+            w = weight * react(*pq)
+            for s in range(2):
+                own = weight * pq[s]
+                at_r = slice(8 + r, 8 + r + ROWS)
+                a[s, z, at_r, :] = a[s, z, at_r, :] + own
+                s1[s, z, r : r + ROWS, :] = rows(s1, s, z, r=r) + (
+                    pq[s] + SIGN[s] * w - DECAY[s] * own
+                )
+
     def sum_two(z, base=True):
         weight = (DT * S[1][0], DT * S[1][1] - H, DT * S[1][2])
         for r in chunks:
@@ -305,6 +327,8 @@
 
     loads[0].wait()
     loads[1].wait()
+    for z in (1, 2, 3, 4):
+        begin_one(z)
     pl.when(has_lo)(lambda: arrived(u.at[2, :, 0], r_h.at[1, 0]))
     pl.when(has_hi)(lambda: arrived(u.at[2, :, 5], r_h.at[1, 1]))
     send(u.at[2, :, 0], u.at[0, :, 0], r_u0h.at[0], nxt, has_lo & has_next)
@@ -313,7 +337,7 @@
     send(u.at[0, :, 4], u.at[0, :, 0], r_u0h.at[0], hi, has_hi & ~has_prior)
     send(u.at[0, :, 1], u.at[0, :, 5], r_u0h.at[1], lo, has_lo & ~has_prior)
     for z in (1, 2, 3, 4):
-        sum_one(z)
+        end_one(z)
     edges = ((0, 1, 2, 0), (1, 4, 3, 5))
     for k, z, inner, _ in edges:
         for r in chunks:

time: 46 us -> 45.9 us (level)
  no operation moved by 1% of the time
where the time goes in v6:
time: 45.9 us; the launch traced here: 45.7 us
  Pallas kernels  44.8 us (98%)
  local copies, waits for them, and re-layouts  0.97 us (2%)
    pallas_call x1, Pallas kernels, local(): pl.pallas_call(functools.partial(kernel, shape), out_shape=jax.ShapeDtype...  44.8 us
    unnamed x1, local copies, waits for them, and re-layouts  0.97 us

profile of v6, /device:TPU:384, one launch (start us, length us, event | category | flops | bytes accessed | tf_op | source)
XLA Modules:
  0.0 45.7 jit_solution(7662466127907032437)
XLA Ops:
  0.0 44.8 %iteration.1 = f32[1,2,2,4,128,128]{5,4,3,2,1,0:T(8,128)S(1)} custom-call(f32[1,2,2,4,128,128]{5,4,3,2,1,0:T(8,128)} %nodes.1, f32[2,4,128,128]{3,2,1,0:T(8,128)} %initial.1, bf16[2,128,256]{2,1,0:T(8,128)(2,1)} %constant.14.clone.fx_h, bf16[2,256,128]{2,1,0:T(8,128)(2,1)} %constant.15.clone.fy_h, bf16[2,64,128]{2,1,0:T(8,128)(2,1)} %constant.16.clone.mz_h, ...), custom_call_target="tpu_custom_call" | custom-call | tf_op jit(solution)/shard_map/iteration/pallas_call | solution.py:635
  44.8 1.0 %copy.11 = f32[1,2,2,4,128,128]{5,4,3,2,1,0:T(8,128)} copy(f32[1,2,2,4,128,128]{5,4,3,2,1,0:T(8,128)S(1)} %iteration.1) | data formatting | bytes 2097152

commit v7 on v6

--- a/solution.py
+++ b/solution.py
@@ -17,7 +17,7 @@
 DT = 0.5
 H = 0.25
 S = ((5.0 / 24.0, 1.0 / 3.0, -1.0 / 24.0), (-1.0 / 24.0, 1.0 / 3.0, 5.0 / 24.0))
-ROWS = 32
+ROWS = 16
 
 
 def sine_table(points, modes, stretch):

time: 45.9 us -> 45.9 us (level)
  no operation moved by 1% of the time
where the time goes in v7:
time: 45.9 us; the launch traced here: 45.7 us
  Pallas kernels  44.8 us (98%)
  local copies, waits for them, and re-layouts  0.97 us (2%)
    pallas_call x1, Pallas kernels, local(): pl.pallas_call(functools.partial(kernel, shape), out_shape=jax.ShapeDtype...  44.8 us
    unnamed x1, local copies, waits for them, and re-layouts  0.97 us

profile of v7, /device:TPU:384, one launch (start us, length us, event | category | flops | bytes accessed | tf_op | source)
XLA Modules:
  0.0 45.7 jit_solution(5344665828272434599)
XLA Ops:
  0.0 44.8 %iteration.1 = f32[1,2,2,4,128,128]{5,4,3,2,1,0:T(8,128)S(1)} custom-call(f32[1,2,2,4,128,128]{5,4,3,2,1,0:T(8,128)} %nodes.1, f32[2,4,128,128]{3,2,1,0:T(8,128)} %initial.1, bf16[2,128,256]{2,1,0:T(8,128)(2,1)} %constant.14.clone.fx_h, bf16[2,256,128]{2,1,0:T(8,128)(2,1)} %constant.15.clone.fy_h, bf16[2,64,128]{2,1,0:T(8,128)(2,1)} %constant.16.clone.mz_h, ...), custom_call_target="tpu_custom_call" | custom-call | tf_op jit(solution)/shard_map/iteration/pallas_call | solution.py:635
  44.8 1.0 %copy.11 = f32[1,2,2,4,128,128]{5,4,3,2,1,0:T(8,128)} copy(f32[1,2,2,4,128,128]{5,4,3,2,1,0:T(8,128)S(1)} %iteration.1) | data formatting | bytes 2097152
